TPU v7x, 256 devices: a whole 4x4x8 slice. The times are simulated.
256 devices in a mesh: gx: 32 (over y, z), gy: 8 (over x, core).
Axes of the slice: x: 4, y: 4, z: 8, core: 2. Of those that a mesh axis runs over, the one named last changes fastest.
Arguments:
- snapshot: float32 [1, 512, 128, 512], P(None, 'gx', 'gy'), may hold values from -25 to 25
Outputs:
- codes: float32 [1, 512, 128, 512], P(None, 'gx', 'gy')
All inputs are finite; a program needn't handle non-finite values.
Results may differ from a plain program's by a relative error of at most 0.0003.
Values sent between devices are 32-bit elements; how exact they have to be, the bound alone decides.
No kernel may reach another device: no remote copies, remote signals or barrier semaphores. Data moves between devices by JAX's collectives and lax.ppermute only.
A program may use at most 64 MiB of HBM per device.

v0:
```python
import math

import jax
import jax.numpy as jnp
from jax import lax
from jax.sharding import PartitionSpec as P

LEVELS = 2


REL_BOUND = 0.01
TWO_PI = 2.0 * math.pi


def extended_2(block, sides, width):
    for axis, dim in sides:
        count = lax.axis_size(axis)
        forward = [(i, i + 1) for i in range(count - 1)]
        forward.append((count - 1, 0))
        backward = [(target, source) for source, target in forward]
        low = lax.ppermute(
            lax.slice_in_dim(block, block.shape[dim] - width, None, axis=dim), axis, forward
        )
        high = lax.ppermute(lax.slice_in_dim(block, 0, width, axis=dim), axis, backward)
        block = jnp.concatenate([low, block, high], axis=dim)
    return block


def cubic(outer_low, inner_low, inner_high, outer_high):
    return (9.0 * (inner_low + inner_high) - (outer_low + outer_high)) / 16.0


def quantize(values, predicted, error_bound):
    scaled = (values - predicted) / (2.0 * error_bound)
    code_vals = scaled - jnp.sin(TWO_PI * scaled) / TWO_PI
    return (code_vals, predicted + 2.0 * error_bound * code_vals)


def extend_along_x(stacked):
    padded = extended_2(stacked, (("gx", 2),), 2)
    return padded[:, :, 1:]


def extend_along_y(stacked):
    padded = extended_2(stacked, (("gy", 3),), 2)
    return padded[:, :, :, 1:]


def is_target(phase_key, direction, stride):
    for spatial in range(3):
        if spatial < direction and phase_key[spatial] % stride != 0:
            return False
        if spatial == direction and phase_key[spatial] % (2 * stride) != stride:
            return False
        if spatial > direction and phase_key[spatial] % (2 * stride) != 0:
            return False
    return True


def shards(snapshot):
    field_count, cells_x, cells_y, cells_z = snapshot.shape
    period = 2**LEVELS
    blocks = (cells_x // period, cells_y // period, cells_z // period)
    local_max = jnp.max(snapshot, axis=(1, 2, 3))
    local_min = jnp.min(snapshot, axis=(1, 2, 3))
    highest = lax.pmax(local_max, ("gx", "gy"))
    lowest = lax.pmin(local_min, ("gx", "gy"))
    error_bound = (REL_BOUND * (highest - lowest)).reshape(field_count, 1, 1, 1)
    split_field = snapshot.reshape(
        field_count, blocks[0], period, blocks[1], period, blocks[2], period
    )
    split_field = split_field.transpose(2, 4, 6, 0, 1, 3, 5)
    all_phases = [
        (first, second, third)
        for first in range(period)
        for second in range(period)
        for third in range(period)
    ]
    initial = {}
    for phase_key in all_phases:
        initial[phase_key] = split_field[phase_key[0], phase_key[1], phase_key[2]]
    rebuilt = dict(initial)
    code_parts = {}
    for depth_level in range(LEVELS, 0, -1):
        stride = 2 ** (depth_level - 1)
        offsets = (-3 * stride, -stride, stride, 3 * stride)
        for direction in range(3):
            targets = [
                phase_key for phase_key in all_phases if is_target(phase_key, direction, stride)
            ]
            sources = []
            for phase_key in targets:
                for offset in offsets:
                    moved = list(phase_key)
                    moved[direction] = (phase_key[direction] + offset) % period
                    if tuple(moved) not in sources:
                        sources.append(tuple(moved))
            stacked = jnp.stack([rebuilt[source_key] for source_key in sources])
            if direction == 0:
                extended = extend_along_x(stacked)
            elif direction == 1:
                extended = extend_along_y(stacked)
            else:
                extended = jnp.concatenate([stacked[..., -1:], stacked, stacked[..., :2]], axis=4)
            extent = blocks[direction]
            for phase_key in targets:
                terms = []
                for offset in offsets:
                    reached = phase_key[direction] + offset
                    moved = list(phase_key)
                    moved[direction] = reached % period
                    block_shift = reached // period
                    chosen = extended[sources.index(tuple(moved))]
                    terms.append(
                        lax.slice_in_dim(
                            chosen, 1 + block_shift, 1 + block_shift + extent, axis=direction + 1
                        )
                    )
                predicted = cubic(terms[0], terms[1], terms[2], terms[3])
                new_codes, new_values = quantize(initial[phase_key], predicted, error_bound)
                rebuilt[phase_key] = new_values
                code_parts[phase_key] = new_codes
    zero_block = jnp.zeros_like(initial[0, 0, 0])
    assembled = jnp.stack(
        [
            jnp.stack(
                [
                    jnp.stack(
                        [
                            code_parts.get((first, second, third), zero_block)
                            for third in range(period)
                        ]
                    )
                    for second in range(period)
                ]
            )
            for first in range(period)
        ]
    )
    assembled = assembled.transpose(3, 4, 0, 5, 1, 6, 2)
    return assembled.reshape(field_count, cells_x, cells_y, cells_z)


def solution(mesh):
    in_specs = (P(None, "gx", "gy", None),)
    out_specs = P(None, "gx", "gy", None)
    return jax.shard_map(shards, mesh=mesh, in_specs=in_specs, out_specs=out_specs, check_vma=False)
```

profile of v0, /device:TPU:1, one launch (start us, length us, event | category | flops | bytes accessed | tf_op | source)
XLA Modules:
  0.0 271.9 jit_solution(17912699606750488682)
XLA Ops:
  0.0 19.5 %reshape.14 = f32[1,4,4,4,4,128,4]{6,5,4,3,2,1,0:T(8,128)} reshape(f32[1,16,16,512]{3,2,1,0:T(8,128)} %param.1) | data formatting | bytes 1048576 | tf_op jit(solution)/shard_map/reshape | solution.py:69
  19.5 6.1 %slice_reduce_fusion.56 = (f32[4,4,128]{2,1,0:T(4,128)S(1)}, f32[4,4,128]{2,1,0:T(4,128)S(1)}, f32[4,4,128]{2,1,0:T(4,128)S(1)}, f32[4,4,128]{2,1,0:T(4,128)S(1)...) fusion(f32[4,4,4,1,4,4,128]{2,6,1,5,0,4,3:T(8,128)} %bitcast.887), kind=kLoop, calls=%fused_computation.56 | loop fusion | bytes 114688 | tf_op jit(solution)/shard_map/slice | solution.py:81
  25.6 2.5 collective-permute-start
  28.1 6.7 %collective-permute-start.1 = (f32[1,1,2,4,128]{4,3,2,1,0:T(4,128)S(1)}, f32[1,1,2,4,128]{4,3,2,1,0:T(4,128)S(1)}, u32[]{:S(2)}, u32[]{:S(2)}) collective-permute-start(f32[1,1,2,4,128]{4,3,2,1,0:T(4,128)S(1)} %get-tuple-element.268), channel_id=1, source_target_pairs={{8,0},{16,8},{24,16},{32,24},{40,32},{48,40},{56,48},{64,56},{72,6... | collective-permute-start | bytes 12296 | tf_op jit(solution)/shard_map/ppermute | solution.py:24
  34.8 13.6 %slice_reduce_fusion.30 = (f32[4,4,128]{2,1,0:T(4,128)S(1)}, f32[4,4,128]{2,1,0:T(4,128)S(1)}, f32[4,4,128]{2,1,0:T(4,128)S(1)}, f32[4,4,128]{2,1,0:T(4,128)S(1)...) fusion(f32[4,4,4,1,4,4,128]{2,6,1,5,0,4,3:T(8,128)} %bitcast.888), kind=kLoop, calls=%fused_computation.30 | loop fusion | bytes 311296 | tf_op jit(solution)/shard_map/slice | solution.py:81
  48.4 8.1 %slice_reduce_fusion.37 = (f32[4,4,128]{2,1,0:T(4,128)S(1)}, f32[4,4,128]{2,1,0:T(4,128)S(1)}, f32[4,4,128]{2,1,0:T(4,128)S(1)}, f32[4,4,128]{2,1,0:T(4,128)S(1)...) fusion(f32[4,4,4,1,4,4,128]{2,6,1,5,0,4,3:T(8,128)S(1)} %bitcas, ...), kind=kLoop, calls=%fused_computation.37 | loop fusion | bytes 311296 | tf_op jit(solution)/shard_map/slice | solution.py:81
  56.5 0.7 fusion.262
  57.2 74.0 %pmax.7 = f32[1]{0:T(128)} all-reduce(f32[1]{0:T(128)} %bitcast.2), channel_id=1, replica_groups=mesh['gx'=32,'gy'=8] {'gx','gy'}, use_global_device_ids=true, to_apply=%region_1.0 | all-reduce | flops 1 | bytes 8 | tf_op jit(solution)/shard_map/pmax | solution.py:66
  131.2 74.3 %pmin.7 = f32[1]{0:T(128)} all-reduce(f32[1]{0:T(128)} %bitcast.3), channel_id=1, replica_groups=mesh['gx'=32,'gy'=8] {'gx','gy'}, use_global_device_ids=true, to_apply=%region_3.0 | all-reduce | flops 1 | bytes 8 | tf_op jit(solution)/shard_map/pmin | solution.py:67
  207.0 1.3 collective-permute-start.2
  208.4 14.4 %slice_reduce_fusion.63 = (f32[4,4,128]{2,1,0:T(4,128)S(1)}, f32[4,4,128]{2,1,0:T(4,128)S(1)}, f32[4,4,128]{2,1,0:T(4,128)S(1)}, f32[4,4,128]{2,1,0:T(4,128)S(1)...) fusion(f32[4,4,4,1,4,4,128]{2,6,1,5,0,4,3:T(8,128)} %bitcast.889), kind=kLoop, calls=%fused_computation.63 | loop fusion | bytes 311296 | tf_op jit(solution)/shard_map/slice | solution.py:81
  224.5 1.0 collective-permute-start.4
  225.4 3.9 %collective-permute-start.5 = (f32[8,1,2,4,128]{4,3,2,1,0:T(4,128)S(1)}, f32[8,1,2,4,128]{4,3,2,1,0:T(4,128)S(1)}, u32[]{:S(2)}, u32[]{:S(2)}) collective-permute-start(f32[8,1,2,4,128]{4,3,2,1,0:T(4,128)S(1)} %get-tuple-element.196), channel_id=1, source_target_pairs={{8,0},{16,8},{24,16},{32,24},{40,32},{48,40},{56,48},{64,56},{72,6... | collective-permute-start | bytes 98312 | tf_op jit(solution)/shard_map/ppermute | solution.py:24
  229.4 1.2 collective-permute-done.4
  232.2 2.9 %collective-permute-start.6 = (f32[16,1,4,2,128]{4,3,2,1,0:T(2,128)S(1)}, f32[16,1,4,2,128]{4,3,2,1,0:T(2,128)S(1)}, u32[]{:S(2)}, u32[]{:S(2)}) collective-permute-start(f32[16,1,4,2,128]{4,3,2,1,0:T(2,128)S(1)} %get-tuple-element.185), channel_id=1, source_target_pairs={{0,1},{1,2},{2,3},{3,4},{4,5},{5,6},{6,7},{7,0},{8,9},{9,10},{10,1... | collective-permute-start | bytes 196616 | tf_op jit(solution)/shard_map/ppermute | solution.py:21
  235.1 0.6 collective-permute-start.7
  235.7 0.7 collective-permute-done.6
  236.5 2.4 collective-permute-done.7
  242.8 0.5 pad_maximum_fusion
  243.6 0.2 subtract_bitcast_fusion.19
  243.8 0.2 subtract_bitcast_fusion.21
  244.0 0.2 subtract_bitcast_fusion.23
  244.3 0.2 subtract_bitcast_fusion.25
  244.5 0.2 subtract_bitcast_fusion.27
  244.7 0.2 subtract_bitcast_fusion.29
  245.0 0.2 subtract_bitcast_fusion.1
  245.2 0.2 subtract_bitcast_fusion.3
  246.2 0.2 subtract_bitcast_fusion.11
  246.6 0.2 subtract_bitcast_fusion.15
  246.8 0.2 subtract_bitcast_fusion.17
  247.4 8.7 %copy.1892 = f32[1,4,4,4,4,128,4]{6,5,4,3,2,1,0:T(8,128)} copy(f32[1,4,4,4,4,128,4]{5,3,1,6,4,0,2:T(4,128)S(1)} %maximum_bitcast_fusion) | data formatting | bytes 1048576 | tf_op jit(solution)/shard_map/transpose | solution.py:140
  256.1 15.7 %reshape.15 = f32[1,16,16,512]{3,2,1,0:T(8,128)} reshape(f32[1,4,4,4,4,128,4]{6,5,4,3,2,1,0:T(8,128)} %copy.1892) | data formatting | bytes 1048576 | tf_op jit(solution)/shard_map/reshape | solution.py:141
  (127 shorter events, 8.9 us)
Async XLA Ops:
  19.5 28.9 %copy-start = (f32[1,4,4,4,4,128,4]{6,5,4,3,2,1,0:T(8,128)S(1)}, f32[1,4,4,4,4,128,4]{6,5,4,3,2,1,0:T(8,128)}, u32[]{:S(2)}) copy-start(f32[1,4,4,4,4,128,4]{6,5,4,3,2,1,0:T(8,128)} %reshape.14) | copy-start | bytes 1572868
  25.6 181.2 %collective-permute-start = (f32[1,1,2,4,128]{4,3,2,1,0:T(4,128)S(1)}, f32[1,1,2,4,128]{4,3,2,1,0:T(4,128)S(1)}, u32[]{:S(2)}, u32[]{:S(2)}) collective-permute-start(f32[1,1,2,4,128]{4,3,2,1,0:T(4,128)S(1)} %get-tuple-element.267), channel_id=1, source_target_pairs={{0,8},{8,16},{16,24},{24,32},{32,40},{40,48},{48,56},{56,64},{64,7... | collective-permute-start | bytes 12296 | tf_op jit(solution)/shard_map/ppermute | solution.py:21
  28.1 28.3 %copy-start.1 = (f32[1,16,16,512]{3,2,1,0:T(8,128)S(1)}, f32[1,16,16,512]{3,2,1,0:T(8,128)}, u32[]{:S(2)}) copy-start(f32[1,16,16,512]{3,2,1,0:T(8,128)} %param.1) | copy-start | bytes 1572868
  28.1 178.7 %collective-permute-start.1 = (f32[1,1,2,4,128]{4,3,2,1,0:T(4,128)S(1)}, f32[1,1,2,4,128]{4,3,2,1,0:T(4,128)S(1)}, u32[]{:S(2)}, u32[]{:S(2)}) collective-permute-start(f32[1,1,2,4,128]{4,3,2,1,0:T(4,128)S(1)} %get-tuple-element.268), channel_id=1, source_target_pairs={{8,0},{16,8},{24,16},{32,24},{40,32},{48,40},{56,48},{64,56},{72,6... | collective-permute-start | bytes 12296 | tf_op jit(solution)/shard_map/ppermute | solution.py:24
  207.0 15.7 %collective-permute-start.2 = (f32[2,1,4,2,128]{4,3,2,1,0:T(2,128)S(1)}, f32[2,1,4,2,128]{4,3,2,1,0:T(2,128)S(1)}, u32[]{:S(2)}, u32[]{:S(2)}) collective-permute-start(f32[2,1,4,2,128]{4,3,2,1,0:T(2,128)S(1)} %get-tuple-element.263), channel_id=1, source_target_pairs={{0,1},{1,2},{2,3},{3,4},{4,5},{5,6},{6,7},{7,0},{8,9},{9,10},{10,1... | collective-permute-start | bytes 24584 | tf_op jit(solution)/shard_map/ppermute | solution.py:21
  208.4 14.4 %collective-permute-start.3 = (f32[2,1,4,2,128]{4,3,2,1,0:T(2,128)S(1)}, f32[2,1,4,2,128]{4,3,2,1,0:T(2,128)S(1)}, u32[]{:S(2)}, u32[]{:S(2)}) collective-permute-start(f32[2,1,4,2,128]{4,3,2,1,0:T(2,128)S(1)} %get-tuple-element.264), channel_id=1, source_target_pairs={{1,0},{2,1},{3,2},{4,3},{5,4},{6,5},{7,6},{0,7},{9,8},{10,9},{11,1... | collective-permute-start | bytes 24584 | tf_op jit(solution)/shard_map/ppermute | solution.py:24
  224.5 6.2 %collective-permute-start.4 = (f32[8,1,2,4,128]{4,3,2,1,0:T(4,128)S(1)}, f32[8,1,2,4,128]{4,3,2,1,0:T(4,128)S(1)}, u32[]{:S(2)}, u32[]{:S(2)}) collective-permute-start(f32[8,1,2,4,128]{4,3,2,1,0:T(4,128)S(1)} %get-tuple-element.195), channel_id=1, source_target_pairs={{0,8},{8,16},{16,24},{24,32},{32,40},{40,48},{48,56},{56,64},{64,7... | collective-permute-start | bytes 98312 | tf_op jit(solution)/shard_map/ppermute | solution.py:21
  225.4 5.2 %collective-permute-start.5 = (f32[8,1,2,4,128]{4,3,2,1,0:T(4,128)S(1)}, f32[8,1,2,4,128]{4,3,2,1,0:T(4,128)S(1)}, u32[]{:S(2)}, u32[]{:S(2)}) collective-permute-start(f32[8,1,2,4,128]{4,3,2,1,0:T(4,128)S(1)} %get-tuple-element.196), channel_id=1, source_target_pairs={{8,0},{16,8},{24,16},{32,24},{40,32},{48,40},{56,48},{64,56},{72,6... | collective-permute-start | bytes 98312 | tf_op jit(solution)/shard_map/ppermute | solution.py:24
  232.2 4.2 %collective-permute-start.6 = (f32[16,1,4,2,128]{4,3,2,1,0:T(2,128)S(1)}, f32[16,1,4,2,128]{4,3,2,1,0:T(2,128)S(1)}, u32[]{:S(2)}, u32[]{:S(2)}) collective-permute-start(f32[16,1,4,2,128]{4,3,2,1,0:T(2,128)S(1)} %get-tuple-element.185), channel_id=1, source_target_pairs={{0,1},{1,2},{2,3},{3,4},{4,5},{5,6},{6,7},{7,0},{8,9},{9,10},{10,1... | collective-permute-start | bytes 196616 | tf_op jit(solution)/shard_map/ppermute | solution.py:21
  235.1 3.7 %collective-permute-start.7 = (f32[16,1,4,2,128]{4,3,2,1,0:T(2,128)S(1)}, f32[16,1,4,2,128]{4,3,2,1,0:T(2,128)S(1)}, u32[]{:S(2)}, u32[]{:S(2)}) collective-permute-start(f32[16,1,4,2,128]{4,3,2,1,0:T(2,128)S(1)} %get-tuple-element.186), channel_id=1, source_target_pairs={{1,0},{2,1},{3,2},{4,3},{5,4},{6,5},{7,6},{0,7},{9,8},{10,9},{11,1... | collective-permute-start | bytes 196616 | tf_op jit(solution)/shard_map/ppermute | solution.py:24
where the time goes:
time: 273 us; the launch traced here: 272 us
  blocking collectives  148 us (54%)
  local copies, waits for them, and re-layouts  86.6 us (32%)
  starting transfers between devices  18.9 us (7%)
  other arithmetic  11.9 us (4%)
  waiting for transfers between devices  4.33 us (2%)
    pmin x1, blocking collectives, shards(): lowest = lax.pmin(local_min, ('gx', 'gy'))  74.3 us
    pmax x1, blocking collectives, shards(): highest = lax.pmax(local_max, ('gx', 'gy'))  74 us
    slice x4, local copies, waits for them, and re-layouts, shards(): initial[phase_key] = split_field[phase_key[0], phase_key[1], phase_key[2]]  42.1 us
    reshape x1, local copies, waits for them, and re-layouts, shards(): snapshot.reshape(field_count, blocks[0], period, blocks[1], period, block...  19.5 us
    reshape x1, local copies, waits for them, and re-layouts, shards(): return assembled.reshape(field_count, cells_x, cells_y, cells_z)  15.7 us
    ppermute x4, starting transfers between devices, extended_2(): lax.ppermute(lax.slice_in_dim(block, 0, width, axis=dim), axis, backward)  11.2 us
    transpose x1, local copies, waits for them, and re-layouts, shards(): assembled = assembled.transpose(3, 4, 0, 5, 1, 6, 2)  8.71 us
    ppermute x4, starting transfers between devices, extended_2(): lax.ppermute(lax.slice_in_dim(block, block.shape[dim] - width, None, axis...  7.73 us
  transfers between devices with their start and end apart: 8, of which 3 were waited for; matrix products, arithmetic and copies ran while one was open for 14% of the time, Pallas kernels for 0%

commit v1 on v0

v1 whole, which is shorter than its diff:
```python
import math

import jax
import jax.numpy as jnp
from jax import lax
from jax.experimental import pallas as pl
from jax.experimental.pallas import tpu as pltpu
from jax.sharding import PartitionSpec as P

REL_BOUND = 0.01
AXES = ("gx", "gy")

Q_COEFFS = (6.579714775085449, -12.986868858337402, 12.191614151000977, -6.570947170257568, 1.9706368446350098)

PLANES = 33
ROWS = 24
OWN_X = 8
OWN_R = 8
PAIRS = 8

LOW_X = (8, 12, 14)
HIGH_X = (0, 2, 4, 8)
LOW_TILES = ((0, 8), (0, 12), (0, 14), (1, 14))
HIGH_TILES = ((0, 0), (0, 2), (1, 0), (1, 2), (0, 4), (0, 8))


def lane_index():
    return lax.broadcasted_iota(jnp.int32, (8, 128), 1)


def swap_stage(first, second, keep, width):
    merged = jnp.where(keep, first, pltpu.roll(second, width, 1))
    other = jnp.where(keep, pltpu.roll(first, 128 - width, 1), second)
    return merged, other


def block_transpose(parts, lane):
    low_half = lane < 64
    low_quarter = (lane % 64) < 32
    a0, a2 = swap_stage(parts[0], parts[2], low_half, 64)
    a1, a3 = swap_stage(parts[1], parts[3], low_half, 64)
    b0, b1 = swap_stage(a0, a1, low_quarter, 32)
    b2, b3 = swap_stage(a2, a3, low_quarter, 32)
    return b0, b1, b2, b3


def split_phases(chunks, lane):
    order = 4 * (lane % 32) + lane // 32
    sorted_chunks = [jnp.take_along_axis(c, order, axis=1) for c in chunks]
    return block_transpose(sorted_chunks, lane)


def merge_phases(phases, lane):
    order = 32 * (lane % 4) + lane // 4
    blocks = block_transpose(phases, lane)
    return [jnp.take_along_axis(b, order, axis=1) for b in blocks]


def prepare_kernel(block_ref, even_ref, odd_ref, rest_ref, low_ref, high_ref, peak_ref, scratch):
    lane = lane_index()
    highest = None
    lowest = None
    for x in range(16):
        for t in range(2):
            chunks = [block_ref[x, 8 * t : 8 * t + 8, 128 * k : 128 * k + 128] for k in range(4)]
            top = jnp.maximum(jnp.maximum(chunks[0], chunks[1]), jnp.maximum(chunks[2], chunks[3]))
            low = jnp.minimum(jnp.minimum(chunks[0], chunks[1]), jnp.minimum(chunks[2], chunks[3]))
            highest = top if highest is None else jnp.maximum(highest, top)
            lowest = low if lowest is None else jnp.minimum(lowest, low)
            phases = split_phases(chunks, lane)
            rest_ref[0, x, 8 * t : 8 * t + 8, :] = phases[1]
            rest_ref[1, x, 8 * t : 8 * t + 8, :] = phases[3]
            scratch[0, x, 8 * t : 8 * t + 8, :] = phases[0]
            scratch[1, x, 8 * t : 8 * t + 8, :] = phases[2]
    for x in range(16):
        for z in range(2):
            even_ref[z, x] = scratch[z, x, pl.ds(0, 8, stride=2), :]
            odd_ref[z, x] = scratch[z, x, pl.ds(1, 8, stride=2), :]
    for i, (z, x) in enumerate(LOW_TILES):
        low_ref[i] = even_ref[z, x]
    for i, (z, x) in enumerate(HIGH_TILES):
        high_ref[i] = even_ref[z, x]
    peak = jnp.where(lax.broadcasted_iota(jnp.int32, (1, 128), 1) < 64, jnp.max(highest), -jnp.min(lowest))
    peak_ref[...] = jnp.broadcast_to(peak, peak_ref.shape)


def code_of(scaled):
    whole = jnp.round(scaled)
    r = scaled - whole
    s = r * r
    q = Q_COEFFS[-1]
    for c in Q_COEFFS[-2::-1]:
        q = q * s + c
    return whole + (r * s) * q


def compress_kernel(
    even_ref, odd_ref, rest_ref, ylow_ref, yhigh_ref, xlow_ref, xhigh_ref, ll_ref, lh_ref, hl_ref, hh_ref,
    peaks_ref, out_ref, known0, known2, codes0, codes2, full0, full2, fullc0, fullc2,
):
    lane = lane_index()
    known = (known0, known2)
    codes = (codes0, codes2)
    full = (full0, full2)
    fullc = (fullc0, fullc2)

    def plane(x):
        return (x + OWN_X) * ROWS

    for z in range(2):
        for x in range(16):
            base = plane(x)
            known[z][base : base + 8, :] = ylow_ref[z, x]
            known[z][base + 8 : base + 16, :] = even_ref[z, x]
            known[z][base + 16 : base + 24, :] = yhigh_ref[z, x]
    for i, (z, x) in enumerate(LOW_TILES):
        base = plane(x - 16)
        known[z][base : base + 8, :] = ll_ref[i]
        known[z][base + 8 : base + 16, :] = xlow_ref[i]
        known[z][base + 16 : base + 24, :] = lh_ref[i]
    for i, (z, x) in enumerate(HIGH_TILES):
        base = plane(x + 16)
        known[z][base : base + 8, :] = hl_ref[i]
        known[z][base + 8 : base + 16, :] = xhigh_ref[i]
        known[z][base + 16 : base + 24, :] = hh_ref[i]

    peaks = peaks_ref[0:8, :]
    for i in range(1, peaks_ref.shape[0] // 8):
        peaks = jnp.maximum(peaks, peaks_ref[8 * i : 8 * i + 8, :])
    upper = jnp.max(jnp.where(lane < 64, peaks, -jnp.inf))
    lower = jnp.max(jnp.where(lane < 64, -jnp.inf, peaks))
    step = jnp.full((1, 1), 2.0 * (REL_BOUND * (upper + lower)), jnp.float32)
    inverse = 1.0 / step

    def quantize(values, outer_low, inner_low, inner_high, outer_high):
        predicted = 0.5625 * (inner_low + inner_high) - 0.0625 * (outer_low + outer_high)
        code = code_of((values - predicted) * inverse)
        return code, predicted + step * code

    for x in range(-2, 19, 4):
        rows = [plane(x + d) + OWN_R - 4 for d in (0, -6, -2, 2, 6)]
        args = [known0[pl.ds(r, 8, stride=2), :] for r in rows]
        code, value = quantize(*args)
        known0[pl.ds(rows[0], 8, stride=2), :] = value
        codes0[pl.ds(rows[0], 8, stride=2), :] = code
    rows = [plane(-2 + d) + OWN_R + 12 for d in (0, -6, -2, 2, 6)]
    args = [known0[pl.ds(r, 6, stride=4 * ROWS), :] for r in rows]
    code, value = quantize(*args)
    known0[pl.ds(rows[0], 6, stride=4 * ROWS), :] = value

    for x in range(-2, 19, 2):
        first = plane(x) + OWN_R - 1
        args = [known0[pl.ds(first + d, 6, stride=2), :] for d in (0, -3, -1, 1, 3)]
        code, value = quantize(*args)
        known0[pl.ds(first, 6, stride=2), :] = value
        codes0[pl.ds(first, 6, stride=2), :] = code

    for x in range(-2, 19, 2):
        for first, count in ((OWN_R - 1, 8), (OWN_R + 7, 3)):
            rows = pl.ds(plane(x) + first, count)
            k = known0[rows, :]
            code, value = quantize(
                known2[rows, :], pltpu.roll(k, 1, 1), k, pltpu.roll(k, 127, 1), pltpu.roll(k, 126, 1)
            )
            known2[rows, :] = value
            codes2[rows, :] = code
    for x in range(0, 16, 4):
        codes0[pl.ds(plane(x) + OWN_R, 4, stride=2), :] = jnp.zeros((4, 128), jnp.float32)

    for x in range(1, 16, 2):
        for first, count in ((OWN_R - 1, 8), (OWN_R + 7, 3)):
            for z in range(2):
                args = [known[z][pl.ds(plane(x + d) + first, count), :] for d in (0, -3, -1, 1, 3)]
                code, value = quantize(*args)
                known[z][pl.ds(plane(x) + first, count), :] = value
                codes[z][pl.ds(plane(x) + first, count), :] = code

    for x in range(16):
        for z in range(2):
            base = plane(x) + OWN_R
            inner = known[z][pl.ds(base, 8), :]
            code, value = quantize(
                odd_ref[z, x],
                known[z][pl.ds(base - 1, 8), :],
                inner,
                known[z][pl.ds(base + 1, 8), :],
                known[z][pl.ds(base + 2, 8), :],
            )
            full[z][x, pl.ds(0, 8, stride=2), :] = inner
            full[z][x, pl.ds(1, 8, stride=2), :] = value
            fullc[z][x, pl.ds(0, 8, stride=2), :] = codes[z][pl.ds(base, 8), :]
            fullc[z][x, pl.ds(1, 8, stride=2), :] = code
        for t in range(2):
            rows = slice(8 * t, 8 * t + 8)
            k0 = full0[x, rows, :]
            k2 = full2[x, rows, :]
            k0_next = pltpu.roll(k0, 127, 1)
            k2_next = pltpu.roll(k2, 127, 1)
            k2_last = pltpu.roll(k2, 1, 1)
            code1, _ = quantize(rest_ref[0, x, rows, :], k2_last, k0, k2, k0_next)
            code3, _ = quantize(rest_ref[1, x, rows, :], k0, k2, k0_next, k2_next)
            merged = merge_phases([fullc0[x, rows, :], code1, fullc2[x, rows, :], code3], lane)
            for k in range(4):
                out_ref[x, rows, 128 * k : 128 * k + 128] = merged[k]


def shards(snapshot):
    nx = lax.axis_size("gx")
    ny = lax.axis_size("gy")
    f32 = jnp.float32
    vmem = pl.BlockSpec(memory_space=pltpu.VMEM)
    block = snapshot.reshape(snapshot.shape[1:])
    shape = jax.ShapeDtypeStruct
    even, odd, rest, low, high, peak = pl.pallas_call(
        prepare_kernel,
        in_specs=[vmem],
        out_specs=[vmem] * 6,
        out_shape=[
            shape((2, 16, 8, 128), f32),
            shape((2, 16, 8, 128), f32),
            shape((2, 16, 16, 128), f32),
            shape((len(LOW_TILES), 8, 128), f32),
            shape((len(HIGH_TILES), 8, 128), f32),
            shape((nx * ny, 128), f32),
        ],
        scratch_shapes=[pltpu.VMEM((2, 16, 16, 128), f32)],
        compiler_params=pltpu.CompilerParams(vmem_limit_bytes=16 * 1024 * 1024),
        name="prepare",
    )(block)

    def shifted(array, dx, dy):
        pairs = []
        for x in range(nx):
            for y in range(ny):
                pairs.append((x * ny + y, (x + dx) % nx * ny + (y + dy) % ny))
        return lax.ppermute(array, AXES, pairs)

    ylow = shifted(even, 0, 1)
    yhigh = shifted(even, 0, -1)
    xlow = shifted(low, 1, 0)
    xhigh = shifted(high, -1, 0)
    ll = shifted(low, 1, 1)
    lh = shifted(low, 1, -1)
    hl = shifted(high, -1, 1)
    hh = shifted(high, -1, -1)
    peaks = lax.all_to_all(peak, AXES, 0, 0, tiled=True)

    codes = pl.pallas_call(
        compress_kernel,
        in_specs=[vmem] * 12,
        out_specs=vmem,
        out_shape=shape(block.shape, f32),
        scratch_shapes=[pltpu.VMEM((PLANES * ROWS, 128), f32)] * 4 + [pltpu.VMEM((16, 16, 128), f32)] * 4,
        compiler_params=pltpu.CompilerParams(vmem_limit_bytes=24 * 1024 * 1024),
        name="compress",
    )(even, odd, rest, ylow, yhigh, xlow, xhigh, ll, lh, hl, hh, peaks)
    return codes.reshape(snapshot.shape)


def solution(mesh):
    spec = P(None, "gx", "gy", None)
    return jax.shard_map(shards, mesh=mesh, in_specs=(spec,), out_specs=spec, check_vma=False)
```

time: 273 us -> 42.1 us (0.15)
  the two profiles are of different devices: /device:TPU:1 before, /device:TPU:7 now
where the time goes in v1:
time: 42.1 us; the launch traced here: 41.9 us
  starting transfers between devices  31.8 us (76%)
  Pallas kernels  5.17 us (12%)
  waiting for transfers between devices  3.85 us (9%)
  local copies, waits for them, and re-layouts  1.04 us (2%)
    ppermute x8, starting transfers between devices, shifted(): return lax.ppermute(array, AXES, pairs)  16.9 us
    all_to_all x1, starting transfers between devices, shards(): peaks = lax.all_to_all(peak, AXES, 0, 0, tiled=True)  14.9 us
    ppermute x8, waiting for transfers between devices, shifted(): return lax.ppermute(array, AXES, pairs)  3.85 us
    pallas_call x1, Pallas kernels, shards(): pl.pallas_call(prepare_kernel, in_specs=[vmem], out_specs=[vmem] * 6, out...  3.31 us
    pallas_call x1, Pallas kernels, shards(): pl.pallas_call(compress_kernel, in_specs=[vmem] * 12, out_specs=vmem, out...  1.86 us
    unnamed x2, local copies, waits for them, and re-layouts  1.04 us
  transfers between devices with their start and end apart: 9, of which 2 were waited for; matrix products, arithmetic and copies ran while one was open for 0% of the time, Pallas kernels for 0%

profile of v1, /device:TPU:7, one launch (start us, length us, event | category | flops | bytes accessed | tf_op | source)
XLA Modules:
  0.0 41.9 jit_solution(12933096196915819421)
XLA Ops:
  0.0 0.0 copy-start
  0.0 1.0 %copy-done = f32[1,16,16,512]{3,2,1,0:T(8,128)S(1)} copy-done((f32[1,16,16,512]{3,2,1,0:T(8,128)S(1)}, f32[1,16,16,512]{3,2,1,0:T(8,128)}, u32[]{:S(2)}) %copy-start) | copy-done | bytes 524312
  1.0 3.3 %prepare.1 = (f32[2,16,8,128]{3,2,1,0:T(8,128)S(1)}, f32[2,16,8,128]{3,2,1,0:T(8,128)S(1)}, f32[2,16,16,128]{3,2,1,0:T(8,128)S(1)}, f32[4,8,128]{2,1,0:T(8,128)S...) custom-call(f32[16,16,512]{2,1,0:T(8,128)S(1)} %bitcast.7), custom_call_target="tpu_custom_call" | custom-call | tf_op jit(solution)/shard_map/prepare/pallas_call | solution.py:214
  4.4 14.9 %all-to-all-start = ((f32[256,1,128]{2,1,0:T(1,128)}), f32[256,1,128]{2,1,0:T(1,128)S(1)}, u32[]{:S(2)}, u32[]{:S(2)}) async-start(f32[256,1,128]{2,1,0:T(1,128)} %bitcast.2), calls=%async_computation | async-start | bytes 262144 | tf_op jit(solution)/shard_map/all_to_all | solution.py:246
  19.3 0.4 collective-permute-start.1
  19.7 2.6 %collective-permute-start = (f32[2,16,8,128]{3,2,1,0:T(8,128)S(1)}, f32[2,16,8,128]{3,2,1,0:T(8,128)S(1)}, u32[]{:S(2)}, u32[]{:S(2)}) collective-permute-start(f32[2,16,8,128]{3,2,1,0:T(8,128)S(1)} %get-tuple-element.11.even_ref), channel_id=1, source_target_pairs={{0,1},{1,2},{2,3},{3,4},{4,5},{5,6},{6,7},{7,0},{8,9},{9,10},{10,1... | collective-permute-start | bytes 393224 | tf_op jit(solution)/shard_map/ppermute | solution.py:236
  22.3 0.0 collective-permute-start.5
  22.3 5.2 %collective-permute-start.4 = (f32[4,8,128]{2,1,0:T(8,128)S(1)}, f32[4,8,128]{2,1,0:T(8,128)S(1)}, u32[]{:S(2)}, u32[]{:S(2)}) collective-permute-start(f32[4,8,128]{2,1,0:T(8,128)S(1)} %get-tuple-element.14), channel_id=1, source_target_pairs={{0,9},{1,10},{2,11},{3,12},{4,13},{5,14},{6,15},{7,8},{8,17},{9,18... | collective-permute-start | bytes 49160 | tf_op jit(solution)/shard_map/ppermute | solution.py:236
  27.5 1.5 %collective-permute-start.2 = (f32[4,8,128]{2,1,0:T(8,128)S(1)}, f32[4,8,128]{2,1,0:T(8,128)S(1)}, u32[]{:S(2)}, u32[]{:S(2)}) collective-permute-start(f32[4,8,128]{2,1,0:T(8,128)S(1)} %get-tuple-element.14), channel_id=1, source_target_pairs={{0,8},{1,9},{2,10},{3,11},{4,12},{5,13},{6,14},{7,15},{8,16},{9,17... | collective-permute-start | bytes 49160 | tf_op jit(solution)/shard_map/ppermute | solution.py:236
  28.9 2.1 %collective-permute-done.5.lh_ref = f32[4,8,128]{2,1,0:T(8,128)S(1)} collective-permute-done((f32[4,8,128]{2,1,0:T(8,128)S(1)}, f32[4,8,128]{2,1,0:T(8,128)S(1)}, u32[]{:S(2)}, u32[]{:S(2)}) %collective-permute-start.5) | collective-permute-done | bytes 16416 | tf_op jit(solution)/shard_map/ppermute | solution.py:236
  31.0 0.4 collective-permute-start.7
  31.4 0.0 collective-permute-done.4.ll_ref
  31.4 6.0 %collective-permute-start.6 = (f32[6,8,128]{2,1,0:T(8,128)S(1)}, f32[6,8,128]{2,1,0:T(8,128)S(1)}, u32[]{:S(2)}, u32[]{:S(2)}) collective-permute-start(f32[6,8,128]{2,1,0:T(8,128)S(1)} %get-tuple-element.15), channel_id=1, source_target_pairs={{0,249},{1,250},{2,251},{3,252},{4,253},{5,254},{6,255},{7,248},{8... | collective-permute-start | bytes 73736 | tf_op jit(solution)/shard_map/ppermute | solution.py:236
  37.4 0.0 collective-permute-done.2.xlow_ref
  37.4 0.9 %collective-permute-start.3 = (f32[6,8,128]{2,1,0:T(8,128)S(1)}, f32[6,8,128]{2,1,0:T(8,128)S(1)}, u32[]{:S(2)}, u32[]{:S(2)}) collective-permute-start(f32[6,8,128]{2,1,0:T(8,128)S(1)} %get-tuple-element.15), channel_id=1, source_target_pairs={{0,248},{1,249},{2,250},{3,251},{4,252},{5,253},{6,254},{7,255},{8... | collective-permute-start | bytes 73736 | tf_op jit(solution)/shard_map/ppermute | solution.py:236
  38.3 0.0 collective-permute-done.7.hh_ref
  38.3 0.0 collective-permute-done.6.hl_ref
  38.3 1.7 %collective-permute-done.3.xhigh_ref = f32[6,8,128]{2,1,0:T(8,128)S(1)} collective-permute-done((f32[6,8,128]{2,1,0:T(8,128)S(1)}, f32[6,8,128]{2,1,0:T(8,128)S(1)}, u32[]{:S(2)}, u32[]{:S(2)}) %collective-permute-start.3) | collective-permute-done | bytes 24608 | tf_op jit(solution)/shard_map/ppermute | solution.py:236
  40.0 0.0 collective-permute-done.1.yhigh_ref
  40.0 0.0 collective-permute-done.ylow_ref
  40.0 0.0 all-to-all-done
  40.0 1.9 %compress.1 = f32[16,16,512]{2,1,0:T(8,128)} custom-call(f32[2,16,8,128]{3,2,1,0:T(8,128)S(1)} %get-tuple-element.11.even_ref, f32[2,16,8,128]{3,2,1,0:T(8,128)S(1)} %get-tuple-element.12.odd_ref, f32[2,16,16,128]{3,2,1,0:T(8,128)S(1)} %get-tuple-element.13.rest_ref, f32[2,16,8,128]{3,2,1,0:T(8,128)S(1)} %collective-permute-done.ylow_ref, ...), custom_call_target="tpu_custom_call" | custom-call | tf_op jit(solution)/shard_map/compress/pallas_call | solution.py:248
Async XLA Ops:
  0.0 1.0 %copy-start = (f32[1,16,16,512]{3,2,1,0:T(8,128)S(1)}, f32[1,16,16,512]{3,2,1,0:T(8,128)}, u32[]{:S(2)}) copy-start(f32[1,16,16,512]{3,2,1,0:T(8,128)} %param.1) | copy-start | bytes 1572868
  4.4 35.7 %all-to-all-start = ((f32[256,1,128]{2,1,0:T(1,128)}), f32[256,1,128]{2,1,0:T(1,128)S(1)}, u32[]{:S(2)}, u32[]{:S(2)}) async-start(f32[256,1,128]{2,1,0:T(1,128)} %bitcast.2), calls=%async_computation | async-start | bytes 262144 | tf_op jit(solution)/shard_map/all_to_all | solution.py:246
  19.3 20.7 %collective-permute-start.1 = (f32[2,16,8,128]{3,2,1,0:T(8,128)S(1)}, f32[2,16,8,128]{3,2,1,0:T(8,128)S(1)}, u32[]{:S(2)}, u32[]{:S(2)}) collective-permute-start(f32[2,16,8,128]{3,2,1,0:T(8,128)S(1)} %get-tuple-element.11.even_ref), channel_id=1, source_target_pairs={{0,7},{1,0},{2,1},{3,2},{4,3},{5,4},{6,5},{7,6},{8,15},{9,8},{10,9... | collective-permute-start | bytes 393224 | tf_op jit(solution)/shard_map/ppermute | solution.py:236
  19.7 20.4 %collective-permute-start = (f32[2,16,8,128]{3,2,1,0:T(8,128)S(1)}, f32[2,16,8,128]{3,2,1,0:T(8,128)S(1)}, u32[]{:S(2)}, u32[]{:S(2)}) collective-permute-start(f32[2,16,8,128]{3,2,1,0:T(8,128)S(1)} %get-tuple-element.11.even_ref), channel_id=1, source_target_pairs={{0,1},{1,2},{2,3},{3,4},{4,5},{5,6},{6,7},{7,0},{8,9},{9,10},{10,1... | collective-permute-start | bytes 393224 | tf_op jit(solution)/shard_map/ppermute | solution.py:236
  22.3 8.7 %collective-permute-start.5 = (f32[4,8,128]{2,1,0:T(8,128)S(1)}, f32[4,8,128]{2,1,0:T(8,128)S(1)}, u32[]{:S(2)}, u32[]{:S(2)}) collective-permute-start(f32[4,8,128]{2,1,0:T(8,128)S(1)} %get-tuple-element.14), channel_id=1, source_target_pairs={{0,15},{1,8},{2,9},{3,10},{4,11},{5,12},{6,13},{7,14},{8,23},{9,16... | collective-permute-start | bytes 49160 | tf_op jit(solution)/shard_map/ppermute | solution.py:236
  22.3 9.1 %collective-permute-start.4 = (f32[4,8,128]{2,1,0:T(8,128)S(1)}, f32[4,8,128]{2,1,0:T(8,128)S(1)}, u32[]{:S(2)}, u32[]{:S(2)}) collective-permute-start(f32[4,8,128]{2,1,0:T(8,128)S(1)} %get-tuple-element.14), channel_id=1, source_target_pairs={{0,9},{1,10},{2,11},{3,12},{4,13},{5,14},{6,15},{7,8},{8,17},{9,18... | collective-permute-start | bytes 49160 | tf_op jit(solution)/shard_map/ppermute | solution.py:236
  27.5 9.9 %collective-permute-start.2 = (f32[4,8,128]{2,1,0:T(8,128)S(1)}, f32[4,8,128]{2,1,0:T(8,128)S(1)}, u32[]{:S(2)}, u32[]{:S(2)}) collective-permute-start(f32[4,8,128]{2,1,0:T(8,128)S(1)} %get-tuple-element.14), channel_id=1, source_target_pairs={{0,8},{1,9},{2,10},{3,11},{4,12},{5,13},{6,14},{7,15},{8,16},{9,17... | collective-permute-start | bytes 49160 | tf_op jit(solution)/shard_map/ppermute | solution.py:236
  31.0 7.3 %collective-permute-start.7 = (f32[6,8,128]{2,1,0:T(8,128)S(1)}, f32[6,8,128]{2,1,0:T(8,128)S(1)}, u32[]{:S(2)}, u32[]{:S(2)}) collective-permute-start(f32[6,8,128]{2,1,0:T(8,128)S(1)} %get-tuple-element.15), channel_id=1, source_target_pairs={{0,255},{1,248},{2,249},{3,250},{4,251},{5,252},{6,253},{7,254},{8... | collective-permute-start | bytes 73736 | tf_op jit(solution)/shard_map/ppermute | solution.py:236
  31.4 6.9 %collective-permute-start.6 = (f32[6,8,128]{2,1,0:T(8,128)S(1)}, f32[6,8,128]{2,1,0:T(8,128)S(1)}, u32[]{:S(2)}, u32[]{:S(2)}) collective-permute-start(f32[6,8,128]{2,1,0:T(8,128)S(1)} %get-tuple-element.15), channel_id=1, source_target_pairs={{0,249},{1,250},{2,251},{3,252},{4,253},{5,254},{6,255},{7,248},{8... | collective-permute-start | bytes 73736 | tf_op jit(solution)/shard_map/ppermute | solution.py:236
  37.4 2.7 %collective-permute-start.3 = (f32[6,8,128]{2,1,0:T(8,128)S(1)}, f32[6,8,128]{2,1,0:T(8,128)S(1)}, u32[]{:S(2)}, u32[]{:S(2)}) collective-permute-start(f32[6,8,128]{2,1,0:T(8,128)S(1)} %get-tuple-element.15), channel_id=1, source_target_pairs={{0,248},{1,249},{2,250},{3,251},{4,252},{5,253},{6,254},{7,255},{8... | collective-permute-start | bytes 73736 | tf_op jit(solution)/shard_map/ppermute | solution.py:236

commit v2 on v1

v2 whole, which is shorter than its diff:
```python
import jax
import jax.numpy as jnp
from jax import lax
from jax.experimental import pallas as pl
from jax.experimental.pallas import tpu as pltpu
from jax.sharding import PartitionSpec as P

REL_BOUND = 0.01
AXES = ("gx", "gy")

Q_COEFFS = (6.579714775085449, -12.986868858337402, 12.191614151000977, -6.570947170257568, 1.9706368446350098)

PLANES = 33
ROWS = 24
OWN_X = 8
OWN_R = 8

LOW_PLANES = ((0, 8), (0, 12), (0, 14), (1, 14))
HIGH_PLANES = ((0, 0), (0, 2), (1, 0), (1, 2), (0, 4), (0, 8))
LOW_ROWS = ((0, 14, 1), (1, 14, 1), (0, 8, 2), (0, 12, 2))
HIGH_ROWS = ((0, 0, 1), (1, 0, 1), (0, 2, 1), (1, 2, 1), (0, 4, 2), (0, 8, 2))
F32 = jnp.float32
BF16 = jnp.bfloat16


def packed_at(rows):
    at, places = 0, []
    for _, _, step in rows:
        places.append(at)
        at += 16 // step
    return places, at


LOW_AT, LOW_COUNT = packed_at(LOW_ROWS)
HIGH_AT, HIGH_COUNT = packed_at(HIGH_ROWS)


def permute_lanes(values, matrix):
    first = values.astype(BF16)
    rest = values - first.astype(F32)
    second = rest.astype(BF16)
    third = (rest - second.astype(F32)).astype(BF16)
    parts = [jnp.dot(piece, matrix, preferred_element_type=F32) for piece in (first, second, third)]
    return parts[0] + (parts[1] + parts[2])


def prepare_kernel(block_ref, phase_ref, low_ref, high_ref, peak_ref):
    highest = [None] * 4
    lowest = [None] * 4
    for x in range(16):
        for t in range(2):
            for k in range(4):
                chunk = block_ref[x, 8 * t : 8 * t + 8, 128 * k : 128 * k + 128]
                highest[k] = chunk if highest[k] is None else jnp.maximum(highest[k], chunk)
                lowest[k] = chunk if lowest[k] is None else jnp.minimum(lowest[k], chunk)
    upper = jnp.maximum(jnp.maximum(highest[0], highest[1]), jnp.maximum(highest[2], highest[3]))
    lower = -jnp.minimum(jnp.minimum(lowest[0], lowest[1]), jnp.minimum(lowest[2], lowest[3]))
    lane = lax.broadcasted_iota(jnp.int32, (8, 128), 1)
    upper = jnp.maximum(upper, pltpu.roll(upper, 64, 1))
    lower = jnp.maximum(lower, pltpu.roll(lower, 64, 1))
    peak = jnp.where(lane < 64, upper, lower)
    for s in (4, 2, 1):
        peak = jnp.maximum(peak, pltpu.roll(peak, s, 0))
    for i in range(peak_ref.shape[0] // 8):
        peak_ref[8 * i : 8 * i + 8, :] = peak

    source = lax.broadcasted_iota(jnp.int32, (256, 256), 0)
    target = lax.broadcasted_iota(jnp.int32, (256, 256), 1)
    matrix = (source == 4 * (target % 64) + target // 64).astype(F32).astype(BF16)
    halves = [permute_lanes(block_ref[:, :, 256 * h : 256 * h + 256].reshape(256, 256), matrix) for h in range(2)]
    low_half = lax.broadcasted_iota(jnp.int32, (256, 128), 1) < 64
    for j in range(2):
        a = halves[0][:, 128 * j : 128 * j + 128]
        b = halves[1][:, 128 * j : 128 * j + 128]
        phase_ref[2 * j] = jnp.where(low_half, a, pltpu.roll(b, 64, 1))
        phase_ref[2 * j + 1] = jnp.where(low_half, pltpu.roll(a, 64, 1), b)

    for ref, rows, places in ((low_ref, LOW_ROWS, LOW_AT), (high_ref, HIGH_ROWS, HIGH_AT)):
        for (z, y, step), at in zip(rows, places):
            for half in range(2 // step):
                ref[at + 8 * half : at + 8 * half + 8, :] = phase_ref[
                    2 * z, pl.ds(16 * 8 * half + y, 8, stride=16 * step), :
                ]


def join_kernel(phase_ref, ylow_ref, yhigh_ref, low_ref, high_ref):
    for ref, planes in ((low_ref, LOW_PLANES), (high_ref, HIGH_PLANES)):
        for i, (z, x) in enumerate(planes):
            base = ROWS * i
            ref[base + OWN_R : base + OWN_R + 8, :] = phase_ref[2 * z, pl.ds(16 * x, 8, stride=2), :]
            for source, rows, places, shift in ((ylow_ref, LOW_ROWS, LOW_AT, -16), (yhigh_ref, HIGH_ROWS, HIGH_AT, 16)):
                for (zz, y, step), at in zip(rows, places):
                    if zz == z and x % step == 0:
                        r = base + OWN_R + (y + shift) // 2
                        ref[r : r + 1, :] = source[at + x // step : at + x // step + 1, :]


def code_of(scaled):
    whole = jnp.round(scaled)
    r = scaled - whole
    s = r * r
    q = Q_COEFFS[-1]
    for c in Q_COEFFS[-2::-1]:
        q = q * s + c
    return whole + (r * s) * q


def compress_kernel(
    phase_ref, ylow_ref, yhigh_ref, xlow_ref, xhigh_ref, peaks_ref, out_ref,
    known0, known2, codes0, codes2, full0, full2, fullc0, fullc1, fullc2, fullc3,
):
    lane = lax.broadcasted_iota(jnp.int32, (8, 128), 1)
    known = (known0, known2)
    codes = (codes0, codes2)
    full = (full0, full2)
    fullc = (fullc0, fullc2)

    def plane(x):
        return (x + OWN_X) * ROWS

    for z in range(2):
        for x in range(16):
            base = plane(x) + OWN_R
            known[z][base : base + 8, :] = phase_ref[2 * z, pl.ds(16 * x, 8, stride=2), :]
    for source, rows, places, shift in ((ylow_ref, LOW_ROWS, LOW_AT, -16), (yhigh_ref, HIGH_ROWS, HIGH_AT, 16)):
        for (z, y, step), at in zip(rows, places):
            r = plane(0) + OWN_R + (y + shift) // 2
            for half in range(2 // step):
                known[z][pl.ds(r + 8 * half * ROWS, 8, stride=step * ROWS), :] = source[at + 8 * half : at + 8 * half + 8, :]
    for source, planes, shift in ((xlow_ref, LOW_PLANES, -16), (xhigh_ref, HIGH_PLANES, 16)):
        for i, (z, x) in enumerate(planes):
            base = plane(x + shift)
            for t in range(3):
                known[z][base + 8 * t : base + 8 * t + 8, :] = source[ROWS * i + 8 * t : ROWS * i + 8 * t + 8, :]

    peaks = peaks_ref[0:8, :]
    for i in range(1, peaks_ref.shape[0] // 8):
        peaks = jnp.maximum(peaks, peaks_ref[8 * i : 8 * i + 8, :])
    upper = jnp.max(jnp.where(lane < 64, peaks, -jnp.inf))
    lower = jnp.max(jnp.where(lane < 64, -jnp.inf, peaks))
    step = jnp.full((1, 1), 2.0 * (REL_BOUND * (upper + lower)), F32)
    inverse = 1.0 / step

    def quantize(values, outer_low, inner_low, inner_high, outer_high):
        predicted = 0.5625 * (inner_low + inner_high) - 0.0625 * (outer_low + outer_high)
        code = code_of((values - predicted) * inverse)
        return code, predicted + step * code

    for x in range(-2, 19, 4):
        rows = [plane(x + d) + OWN_R - 4 for d in (0, -6, -2, 2, 6)]
        args = [known0[pl.ds(r, 8, stride=2), :] for r in rows]
        code, value = quantize(*args)
        known0[pl.ds(rows[0], 8, stride=2), :] = value
        codes0[pl.ds(rows[0], 8, stride=2), :] = code
    rows = [plane(-2 + d) + OWN_R + 12 for d in (0, -6, -2, 2, 6)]
    args = [known0[pl.ds(r, 6, stride=4 * ROWS), :] for r in rows]
    code, value = quantize(*args)
    known0[pl.ds(rows[0], 6, stride=4 * ROWS), :] = value

    for x in range(-2, 19, 2):
        first = plane(x) + OWN_R - 1
        args = [known0[pl.ds(first + d, 6, stride=2), :] for d in (0, -3, -1, 1, 3)]
        code, value = quantize(*args)
        known0[pl.ds(first, 6, stride=2), :] = value
        codes0[pl.ds(first, 6, stride=2), :] = code

    for x in range(-2, 19, 2):
        for first, count in ((OWN_R - 1, 8), (OWN_R + 7, 3)):
            rows = pl.ds(plane(x) + first, count)
            k = known0[rows, :]
            code, value = quantize(
                known2[rows, :], pltpu.roll(k, 1, 1), k, pltpu.roll(k, 127, 1), pltpu.roll(k, 126, 1)
            )
            known2[rows, :] = value
            codes2[rows, :] = code
    for x in range(0, 16, 4):
        codes0[pl.ds(plane(x) + OWN_R, 4, stride=2), :] = jnp.zeros((4, 128), F32)

    for x in range(1, 16, 2):
        for first, count in ((OWN_R - 1, 8), (OWN_R + 7, 3)):
            for z in range(2):
                args = [known[z][pl.ds(plane(x + d) + first, count), :] for d in (0, -3, -1, 1, 3)]
                code, value = quantize(*args)
                known[z][pl.ds(plane(x) + first, count), :] = value
                codes[z][pl.ds(plane(x) + first, count), :] = code

    for x in range(16):
        for z in range(2):
            base = plane(x) + OWN_R
            inner = known[z][pl.ds(base, 8), :]
            code, value = quantize(
                phase_ref[2 * z, pl.ds(16 * x + 1, 8, stride=2), :],
                known[z][pl.ds(base - 1, 8), :],
                inner,
                known[z][pl.ds(base + 1, 8), :],
                known[z][pl.ds(base + 2, 8), :],
            )
            full[z][pl.ds(16 * x, 8, stride=2), :] = inner
            full[z][pl.ds(16 * x + 1, 8, stride=2), :] = value
            fullc[z][pl.ds(16 * x, 8, stride=2), :] = codes[z][pl.ds(base, 8), :]
            fullc[z][pl.ds(16 * x + 1, 8, stride=2), :] = code
        for t in range(2):
            rows = slice(16 * x + 8 * t, 16 * x + 8 * t + 8)
            k0 = full0[rows, :]
            k2 = full2[rows, :]
            k0_next = pltpu.roll(k0, 127, 1)
            k2_next = pltpu.roll(k2, 127, 1)
            k2_last = pltpu.roll(k2, 1, 1)
            fullc1[rows, :], _ = quantize(phase_ref[1, rows, :], k2_last, k0, k2, k0_next)
            fullc3[rows, :], _ = quantize(phase_ref[3, rows, :], k0, k2, k0_next, k2_next)

    source = lax.broadcasted_iota(jnp.int32, (256, 256), 0)
    target = lax.broadcasted_iota(jnp.int32, (256, 256), 1)
    matrix = (target == 4 * (source % 64) + source // 64).astype(F32).astype(BF16)
    low_half = lax.broadcasted_iota(jnp.int32, (256, 128), 1) < 64
    parts = [fullc0[...], fullc1[...], fullc2[...], fullc3[...]]
    turned = [pltpu.roll(p, 64, 1) for p in parts]
    first = jnp.concatenate(
        [jnp.where(low_half, parts[0], turned[1]), jnp.where(low_half, parts[2], turned[3])], axis=1
    )
    second = jnp.concatenate(
        [jnp.where(low_half, turned[0], parts[1]), jnp.where(low_half, turned[2], parts[3])], axis=1
    )
    out_ref[:, :, 0:256] = permute_lanes(first, matrix).reshape(16, 16, 256)
    out_ref[:, :, 256:512] = permute_lanes(second, matrix).reshape(16, 16, 256)


def shards(snapshot):
    nx = lax.axis_size("gx")
    ny = lax.axis_size("gy")
    vmem = pl.BlockSpec(memory_space=pltpu.VMEM)
    block = snapshot.reshape(snapshot.shape[1:])
    params = pltpu.CompilerParams(vmem_limit_bytes=16 * 1024 * 1024)

    def shape(*dims):
        return jax.ShapeDtypeStruct(dims, F32)

    phases, low, high, peak = pl.pallas_call(
        prepare_kernel,
        in_specs=[vmem],
        out_specs=[vmem] * 4,
        out_shape=[shape(4, 256, 128), shape(LOW_COUNT, 128), shape(HIGH_COUNT, 128), shape(nx * ny, 128)],
        compiler_params=params,
        name="prepare",
    )(block)

    def shifted(array, axis, d):
        n = lax.axis_size(axis)
        return lax.ppermute(array, axis, [(i, (i + d) % n) for i in range(n)])

    peaks = lax.all_to_all(peak, AXES, 0, 0, tiled=True)
    ylow = shifted(low, "gy", 1)
    yhigh = shifted(high, "gy", -1)
    low_planes, high_planes = pl.pallas_call(
        join_kernel,
        in_specs=[vmem] * 3,
        out_specs=[vmem] * 2,
        out_shape=[shape(ROWS * len(LOW_PLANES), 128), shape(ROWS * len(HIGH_PLANES), 128)],
        compiler_params=params,
        cost_estimate=pl.CostEstimate(flops=2 * 10**10, bytes_accessed=10**6, transcendentals=0),
        name="join",
    )(phases, ylow, yhigh)
    xlow = shifted(low_planes, "gx", 1)
    xhigh = shifted(high_planes, "gx", -1)

    codes = pl.pallas_call(
        compress_kernel,
        in_specs=[vmem] * 6,
        out_specs=vmem,
        out_shape=shape(*block.shape),
        scratch_shapes=[pltpu.VMEM((PLANES * ROWS, 128), F32)] * 4 + [pltpu.VMEM((256, 128), F32)] * 6,
        compiler_params=params,
        name="compress",
    )(phases, ylow, yhigh, xlow, xhigh, peaks)
    return codes.reshape(snapshot.shape)


def solution(mesh):
    spec = P(None, "gx", "gy", None)
    return jax.shard_map(shards, mesh=mesh, in_specs=(spec,), out_specs=spec, check_vma=False)
```

time: 42.1 us -> 35.3 us (0.84)
  the two profiles are of different devices: /device:TPU:7 before, /device:TPU:1 now
where the time goes in v2:
time: 35.3 us; the launch traced here: 34.9 us
  starting transfers between devices  24.5 us (69%)
  waiting for transfers between devices  6.29 us (18%)
  Pallas kernels  3 us (8%)
  local copies, waits for them, and re-layouts  1.04 us (3%)
    all_to_all x1, starting transfers between devices, shards(): peaks = lax.all_to_all(peak, AXES, 0, 0, tiled=True)  14.5 us
    ppermute x4, starting transfers between devices, shifted(): return lax.ppermute(array, axis, [(i, (i + d) % n) for i in range(n)])  9.97 us
    ppermute x4, waiting for transfers between devices, shifted(): return lax.ppermute(array, axis, [(i, (i + d) % n) for i in range(n)])  6.29 us
    pallas_call x1, Pallas kernels, shards(): pl.pallas_call(compress_kernel, in_specs=[vmem] * 6, out_specs=vmem, out_...  1.98 us
    unnamed x2, local copies, waits for them, and re-layouts  1.04 us
    pallas_call x1, Pallas kernels, shards(): pl.pallas_call(prepare_kernel, in_specs=[vmem], out_specs=[vmem] * 4, out...  0.99 us
  transfers between devices with their start and end apart: 5, of which 1 were waited for; matrix products, arithmetic and copies ran while one was open for 0% of the time, Pallas kernels for 0%

profile of v2, /device:TPU:1, one launch (start us, length us, event | category | flops | bytes accessed | tf_op | source)
XLA Modules:
  0.0 34.9 jit_solution(14369330006006884985)
XLA Ops:
  0.0 0.0 copy-start
  0.0 1.0 %copy-done = f32[1,16,16,512]{3,2,1,0:T(8,128)S(1)} copy-done((f32[1,16,16,512]{3,2,1,0:T(8,128)S(1)}, f32[1,16,16,512]{3,2,1,0:T(8,128)}, u32[]{:S(2)}) %copy-start) | copy-done | bytes 524312
  1.0 1.0 %prepare.1 = (f32[4,256,128]{2,1,0:T(8,128)S(1)}, f32[48,128]{1,0:T(8,128)S(1)}, f32[80,128]{1,0:T(8,128)S(1)}, f32[256,128]{1,0:T(8,128)}) custom-call(f32[16,16,512]{2,1,0:T(8,128)S(1)} %bitcast.6), custom_call_target="tpu_custom_call" | custom-call | tf_op jit(solution)/shard_map/prepare/pallas_call | solution.py:238
  2.0 3.2 %collective-permute-start.1 = (f32[80,128]{1,0:T(8,128)S(1)}, f32[80,128]{1,0:T(8,128)S(1)}, u32[]{:S(2)}, u32[]{:S(2)}) collective-permute-start(f32[80,128]{1,0:T(8,128)S(1)} %get-tuple-element.13), channel_id=1, source_target_pairs={{0,7},{1,0},{2,1},{3,2},{4,3},{5,4},{6,5},{7,6},{8,15},{9,8},{10,9... | collective-permute-start | bytes 122888 | tf_op jit(solution)/shard_map/ppermute | solution.py:249
  5.3 0.0 collective-permute-start
  5.3 14.5 %all-to-all-start = ((f32[256,1,128]{2,1,0:T(1,128)}), f32[256,1,128]{2,1,0:T(1,128)S(1)}, u32[]{:S(2)}, u32[]{:S(2)}) async-start(f32[256,1,128]{2,1,0:T(1,128)} %bitcast.2), calls=%async_computation | async-start | bytes 262144 | tf_op jit(solution)/shard_map/all_to_all | solution.py:251
  19.8 0.0 collective-permute-done.ylow_ref
  19.8 0.0 collective-permute-done.1.yhigh_ref
  19.9 6.7 %collective-permute-start.3 = (f32[144,128]{1,0:T(8,128)S(1)}, f32[144,128]{1,0:T(8,128)S(1)}, u32[]{:S(2)}, u32[]{:S(2)}) collective-permute-start(f32[144,128]{1,0:T(8,128)S(1)} %get-tuple-element.15), channel_id=1, source_target_pairs={{0,248},{8,0},{16,8},{24,16},{32,24},{40,32},{48,40},{56,48},{64,5... | collective-permute-start | bytes 221192 | tf_op jit(solution)/shard_map/ppermute | solution.py:249
  26.6 0.0 collective-permute-start.2
  26.6 6.3 %collective-permute-done.2.xlow_ref = f32[96,128]{1,0:T(8,128)S(1)} collective-permute-done((f32[96,128]{1,0:T(8,128)S(1)}, f32[96,128]{1,0:T(8,128)S(1)}, u32[]{:S(2)}, u32[]{:S(2)}) %collective-permute-start.2) | collective-permute-done | bytes 49184 | tf_op jit(solution)/shard_map/ppermute | solution.py:249
  32.9 0.0 collective-permute-done.3.xhigh_ref
  32.9 0.0 all-to-all-done
  32.9 2.0 %compress.1 = f32[16,16,512]{2,1,0:T(8,128)} custom-call(f32[4,256,128]{2,1,0:T(8,128)S(1)} %get-tuple-element.11.phase_ref, f32[48,128]{1,0:T(8,128)S(1)} %collective-permute-done.ylow_ref, f32[80,128]{1,0:T(8,128)S(1)} %collective-permute-done.1.yhigh_ref, f32[96,128]{1,0:T(8,128)S(1)} %collective-permute-done.2.xlow_ref, ...), custom_call_target="tpu_custom_call" | custom-call | tf_op jit(solution)/shard_map/compress/pallas_call | solution.py:266
  (1 shorter events, 0.0 us)
Async XLA Ops:
  0.0 1.0 %copy-start = (f32[1,16,16,512]{3,2,1,0:T(8,128)S(1)}, f32[1,16,16,512]{3,2,1,0:T(8,128)}, u32[]{:S(2)}) copy-start(f32[1,16,16,512]{3,2,1,0:T(8,128)} %param.1) | copy-start | bytes 1572868
  2.0 17.8 %collective-permute-start.1 = (f32[80,128]{1,0:T(8,128)S(1)}, f32[80,128]{1,0:T(8,128)S(1)}, u32[]{:S(2)}, u32[]{:S(2)}) collective-permute-start(f32[80,128]{1,0:T(8,128)S(1)} %get-tuple-element.13), channel_id=1, source_target_pairs={{0,7},{1,0},{2,1},{3,2},{4,3},{5,4},{6,5},{7,6},{8,15},{9,8},{10,9... | collective-permute-start | bytes 122888 | tf_op jit(solution)/shard_map/ppermute | solution.py:249
  5.3 14.6 %collective-permute-start = (f32[48,128]{1,0:T(8,128)S(1)}, f32[48,128]{1,0:T(8,128)S(1)}, u32[]{:S(2)}, u32[]{:S(2)}) collective-permute-start(f32[48,128]{1,0:T(8,128)S(1)} %get-tuple-element.12), channel_id=1, source_target_pairs={{0,1},{1,2},{2,3},{3,4},{4,5},{5,6},{6,7},{7,0},{8,9},{9,10},{10,1... | collective-permute-start | bytes 73736 | tf_op jit(solution)/shard_map/ppermute | solution.py:249
  5.3 27.6 %all-to-all-start = ((f32[256,1,128]{2,1,0:T(1,128)}), f32[256,1,128]{2,1,0:T(1,128)S(1)}, u32[]{:S(2)}, u32[]{:S(2)}) async-start(f32[256,1,128]{2,1,0:T(1,128)} %bitcast.2), calls=%async_computation | async-start | bytes 262144 | tf_op jit(solution)/shard_map/all_to_all | solution.py:251
  19.9 13.0 %collective-permute-start.3 = (f32[144,128]{1,0:T(8,128)S(1)}, f32[144,128]{1,0:T(8,128)S(1)}, u32[]{:S(2)}, u32[]{:S(2)}) collective-permute-start(f32[144,128]{1,0:T(8,128)S(1)} %get-tuple-element.15), channel_id=1, source_target_pairs={{0,248},{8,0},{16,8},{24,16},{32,24},{40,32},{48,40},{56,48},{64,5... | collective-permute-start | bytes 221192 | tf_op jit(solution)/shard_map/ppermute | solution.py:249
  26.6 6.3 %collective-permute-start.2 = (f32[96,128]{1,0:T(8,128)S(1)}, f32[96,128]{1,0:T(8,128)S(1)}, u32[]{:S(2)}, u32[]{:S(2)}) collective-permute-start(f32[96,128]{1,0:T(8,128)S(1)} %get-tuple-element.14), channel_id=1, source_target_pairs={{0,8},{8,16},{16,24},{24,32},{32,40},{40,48},{48,56},{56,64},{64,7... | collective-permute-start | bytes 147464 | tf_op jit(solution)/shard_map/ppermute | solution.py:249

commit v3 on v2

--- a/solution.py
+++ b/solution.py
@@ -33,6 +33,37 @@
 
 LOW_AT, LOW_COUNT = packed_at(LOW_ROWS)
 HIGH_AT, HIGH_COUNT = packed_at(HIGH_ROWS)
+
+
+def plane_pieces(planes, total):
+    main, extra = [], []
+    for i, (z, x) in enumerate(planes):
+        if z == 1:
+            main.append((i, z, x, 7, 8, 1))
+            extra.append((i, z, x, 15, 3, 1))
+            continue
+        if x in (0, 2, 14):
+            main.append((i, z, x, 4, 8, 1))
+            main.append((i, z, x, 12, 8, 1))
+        else:
+            main.append((i, z, x, 4, 8, 2))
+        extra.append((i, z, x, 20, 1, 1))
+    at, pieces = 0, []
+    for piece in main + extra:
+        pieces.append(piece + (at,))
+        at += piece[4]
+    assert at <= total
+    return pieces
+
+
+LOW_TOTAL = 88
+HIGH_TOTAL = 80
+LOW_PIECES = plane_pieces(LOW_PLANES, LOW_TOTAL)
+HIGH_PIECES = plane_pieces(HIGH_PLANES, HIGH_TOTAL)
+
+
+def row_slice(first, count, step):
+    return pl.ds(first, count) if step == 1 else pl.ds(first, count, stride=step)
 
 
 def permute_lanes(values, matrix):
@@ -83,8 +114,11 @@
                 ]
 
 
-def join_kernel(phase_ref, ylow_ref, yhigh_ref, low_ref, high_ref):
-    for ref, planes in ((low_ref, LOW_PLANES), (high_ref, HIGH_PLANES)):
+def join_kernel(phase_ref, ylow_ref, yhigh_ref, low_ref, high_ref, low_planes, high_planes):
+    for ref, planes, out, pieces in (
+        (low_planes, LOW_PLANES, low_ref, LOW_PIECES),
+        (high_planes, HIGH_PLANES, high_ref, HIGH_PIECES),
+    ):
         for i, (z, x) in enumerate(planes):
             base = ROWS * i
             ref[base + OWN_R : base + OWN_R + 8, :] = phase_ref[2 * z, pl.ds(16 * x, 8, stride=2), :]
@@ -93,6 +127,8 @@
                     if zz == z and x % step == 0:
                         r = base + OWN_R + (y + shift) // 2
                         ref[r : r + 1, :] = source[at + x // step : at + x // step + 1, :]
+        for i, z, x, first, count, step, at in pieces:
+            out[at : at + count, :] = ref[row_slice(ROWS * i + first, count, step), :]
 
 
 def code_of(scaled):
@@ -127,11 +163,9 @@
             r = plane(0) + OWN_R + (y + shift) // 2
             for half in range(2 // step):
                 known[z][pl.ds(r + 8 * half * ROWS, 8, stride=step * ROWS), :] = source[at + 8 * half : at + 8 * half + 8, :]
-    for source, planes, shift in ((xlow_ref, LOW_PLANES, -16), (xhigh_ref, HIGH_PLANES, 16)):
-        for i, (z, x) in enumerate(planes):
-            base = plane(x + shift)
-            for t in range(3):
-                known[z][base + 8 * t : base + 8 * t + 8, :] = source[ROWS * i + 8 * t : ROWS * i + 8 * t + 8, :]
+    for source, pieces, shift in ((xlow_ref, LOW_PIECES, -16), (xhigh_ref, HIGH_PIECES, 16)):
+        for _, z, x, first, count, step, at in pieces:
+            known[z][row_slice(plane(x + shift) + first, count, step), :] = source[at : at + count, :]
 
     peaks = peaks_ref[0:8, :]
     for i in range(1, peaks_ref.shape[0] // 8):
@@ -255,9 +289,12 @@
         join_kernel,
         in_specs=[vmem] * 3,
         out_specs=[vmem] * 2,
-        out_shape=[shape(ROWS * len(LOW_PLANES), 128), shape(ROWS * len(HIGH_PLANES), 128)],
+        out_shape=[shape(LOW_TOTAL, 128), shape(HIGH_TOTAL, 128)],
+        scratch_shapes=[
+            pltpu.VMEM((ROWS * len(LOW_PLANES), 128), F32),
+            pltpu.VMEM((ROWS * len(HIGH_PLANES), 128), F32),
+        ],
         compiler_params=params,
-        cost_estimate=pl.CostEstimate(flops=2 * 10**10, bytes_accessed=10**6, transcendentals=0),
         name="join",
     )(phases, ylow, yhigh)
     xlow = shifted(low_planes, "gx", 1)

time: 35.3 us -> 33.4 us (0.946)
  the two profiles are of different devices: /device:TPU:1 before, /device:TPU:96 now
where the time goes in v3:
time: 33.4 us; the launch traced here: 33.3 us
  starting transfers between devices  19.4 us (58%)
  waiting for transfers between devices  9.8 us (29%)
  Pallas kernels  3.01 us (9%)
  local copies, waits for them, and re-layouts  1.04 us (3%)
    all_to_all x1, starting transfers between devices, shards(): peaks = lax.all_to_all(peak, AXES, 0, 0, tiled=True)  14 us
    ppermute x4, waiting for transfers between devices, shifted(): return lax.ppermute(array, axis, [(i, (i + d) % n) for i in range(n)])  9.8 us
    ppermute x4, starting transfers between devices, shifted(): return lax.ppermute(array, axis, [(i, (i + d) % n) for i in range(n)])  5.39 us
    pallas_call x1, Pallas kernels, shards(): pl.pallas_call(compress_kernel, in_specs=[vmem] * 6, out_specs=vmem, out_...  1.98 us
    unnamed x2, local copies, waits for them, and re-layouts  1.04 us
    pallas_call x1, Pallas kernels, shards(): pl.pallas_call(prepare_kernel, in_specs=[vmem], out_specs=[vmem] * 4, out...  0.99 us
  transfers between devices with their start and end apart: 5, of which 2 were waited for; matrix products, arithmetic and copies ran while one was open for 0% of the time, Pallas kernels for 0%

profile of v3, /device:TPU:96, one launch (start us, length us, event | category | flops | bytes accessed | tf_op | source)
XLA Modules:
  0.0 33.3 jit_solution(1611013989682380811)
XLA Ops:
  0.0 0.0 copy-start
  0.0 1.0 %copy-done = f32[1,16,16,512]{3,2,1,0:T(8,128)S(1)} copy-done((f32[1,16,16,512]{3,2,1,0:T(8,128)S(1)}, f32[1,16,16,512]{3,2,1,0:T(8,128)}, u32[]{:S(2)}) %copy-start) | copy-done | bytes 524312
  1.0 1.0 %prepare.1 = (f32[4,256,128]{2,1,0:T(8,128)S(1)}, f32[48,128]{1,0:T(8,128)S(1)}, f32[80,128]{1,0:T(8,128)S(1)}, f32[256,128]{1,0:T(8,128)}) custom-call(f32[16,16,512]{2,1,0:T(8,128)S(1)} %bitcast.6), custom_call_target="tpu_custom_call" | custom-call | tf_op jit(solution)/shard_map/prepare/pallas_call | solution.py:272
  2.0 14.0 %all-to-all-start = ((f32[256,1,128]{2,1,0:T(1,128)}), f32[256,1,128]{2,1,0:T(1,128)S(1)}, u32[]{:S(2)}, u32[]{:S(2)}) async-start(f32[256,1,128]{2,1,0:T(1,128)} %bitcast.2), calls=%async_computation | async-start | bytes 262144 | tf_op jit(solution)/shard_map/all_to_all | solution.py:285
  16.1 2.5 %collective-permute-start.1 = (f32[80,128]{1,0:T(8,128)S(1)}, f32[80,128]{1,0:T(8,128)S(1)}, u32[]{:S(2)}, u32[]{:S(2)}) collective-permute-start(f32[80,128]{1,0:T(8,128)S(1)} %get-tuple-element.13), channel_id=1, source_target_pairs={{0,7},{1,0},{2,1},{3,2},{4,3},{5,4},{6,5},{7,6},{8,15},{9,8},{10,9... | collective-permute-start | bytes 122888 | tf_op jit(solution)/shard_map/ppermute | solution.py:283
  18.5 0.0 collective-permute-start
  18.5 4.6 %collective-permute-done.ylow_ref = f32[48,128]{1,0:T(8,128)S(1)} collective-permute-done((f32[48,128]{1,0:T(8,128)S(1)}, f32[48,128]{1,0:T(8,128)S(1)}, u32[]{:S(2)}, u32[]{:S(2)}) %collective-permute-start) | collective-permute-done | bytes 24608 | tf_op jit(solution)/shard_map/ppermute | solution.py:283
  23.1 0.0 collective-permute-done.1.yhigh_ref
  23.2 2.9 %collective-permute-start.2 = (f32[88,128]{1,0:T(8,128)S(1)}, f32[88,128]{1,0:T(8,128)S(1)}, u32[]{:S(2)}, u32[]{:S(2)}) collective-permute-start(f32[88,128]{1,0:T(8,128)S(1)} %get-tuple-element.14), channel_id=1, source_target_pairs={{0,8},{8,16},{16,24},{24,32},{32,40},{40,48},{48,56},{56,64},{64,7... | collective-permute-start | bytes 135176 | tf_op jit(solution)/shard_map/ppermute | solution.py:283
  26.1 0.0 collective-permute-start.3
  26.1 5.2 %collective-permute-done.3.xhigh_ref = f32[80,128]{1,0:T(8,128)S(1)} collective-permute-done((f32[80,128]{1,0:T(8,128)S(1)}, f32[80,128]{1,0:T(8,128)S(1)}, u32[]{:S(2)}, u32[]{:S(2)}) %collective-permute-start.3) | collective-permute-done | bytes 40992 | tf_op jit(solution)/shard_map/ppermute | solution.py:283
  31.3 0.0 collective-permute-done.2.xlow_ref
  31.3 0.0 all-to-all-done
  31.3 2.0 %compress.1 = f32[16,16,512]{2,1,0:T(8,128)} custom-call(f32[4,256,128]{2,1,0:T(8,128)S(1)} %get-tuple-element.11.phase_ref, f32[48,128]{1,0:T(8,128)S(1)} %collective-permute-done.ylow_ref, f32[80,128]{1,0:T(8,128)S(1)} %collective-permute-done.1.yhigh_ref, f32[88,128]{1,0:T(8,128)S(1)} %collective-permute-done.2.xlow_ref, ...), custom_call_target="tpu_custom_call" | custom-call | tf_op jit(solution)/shard_map/compress/pallas_call | solution.py:303
  (1 shorter events, 0.0 us)
Async XLA Ops:
  0.0 1.0 %copy-start = (f32[1,16,16,512]{3,2,1,0:T(8,128)S(1)}, f32[1,16,16,512]{3,2,1,0:T(8,128)}, u32[]{:S(2)}) copy-start(f32[1,16,16,512]{3,2,1,0:T(8,128)} %param.1) | copy-start | bytes 1572868
  2.0 29.3 %all-to-all-start = ((f32[256,1,128]{2,1,0:T(1,128)}), f32[256,1,128]{2,1,0:T(1,128)S(1)}, u32[]{:S(2)}, u32[]{:S(2)}) async-start(f32[256,1,128]{2,1,0:T(1,128)} %bitcast.2), calls=%async_computation | async-start | bytes 262144 | tf_op jit(solution)/shard_map/all_to_all | solution.py:285
  16.1 7.1 %collective-permute-start.1 = (f32[80,128]{1,0:T(8,128)S(1)}, f32[80,128]{1,0:T(8,128)S(1)}, u32[]{:S(2)}, u32[]{:S(2)}) collective-permute-start(f32[80,128]{1,0:T(8,128)S(1)} %get-tuple-element.13), channel_id=1, source_target_pairs={{0,7},{1,0},{2,1},{3,2},{4,3},{5,4},{6,5},{7,6},{8,15},{9,8},{10,9... | collective-permute-start | bytes 122888 | tf_op jit(solution)/shard_map/ppermute | solution.py:283
  18.5 4.6 %collective-permute-start = (f32[48,128]{1,0:T(8,128)S(1)}, f32[48,128]{1,0:T(8,128)S(1)}, u32[]{:S(2)}, u32[]{:S(2)}) collective-permute-start(f32[48,128]{1,0:T(8,128)S(1)} %get-tuple-element.12), channel_id=1, source_target_pairs={{0,1},{1,2},{2,3},{3,4},{4,5},{5,6},{6,7},{7,0},{8,9},{9,10},{10,1... | collective-permute-start | bytes 73736 | tf_op jit(solution)/shard_map/ppermute | solution.py:283
  23.2 8.1 %collective-permute-start.2 = (f32[88,128]{1,0:T(8,128)S(1)}, f32[88,128]{1,0:T(8,128)S(1)}, u32[]{:S(2)}, u32[]{:S(2)}) collective-permute-start(f32[88,128]{1,0:T(8,128)S(1)} %get-tuple-element.14), channel_id=1, source_target_pairs={{0,8},{8,16},{16,24},{24,32},{32,40},{40,48},{48,56},{56,64},{64,7... | collective-permute-start | bytes 135176 | tf_op jit(solution)/shard_map/ppermute | solution.py:283
  26.1 5.2 %collective-permute-start.3 = (f32[80,128]{1,0:T(8,128)S(1)}, f32[80,128]{1,0:T(8,128)S(1)}, u32[]{:S(2)}, u32[]{:S(2)}) collective-permute-start(f32[80,128]{1,0:T(8,128)S(1)} %get-tuple-element.15), channel_id=1, source_target_pairs={{0,248},{8,0},{16,8},{24,16},{32,24},{40,32},{48,40},{56,48},{64,5... | collective-permute-start | bytes 122888 | tf_op jit(solution)/shard_map/ppermute | solution.py:283

commit v4 on v3

--- a/solution.py
+++ b/solution.py
@@ -21,6 +21,11 @@
 HIGH_ROWS = ((0, 0, 1), (1, 0, 1), (0, 2, 1), (1, 2, 1), (0, 4, 2), (0, 8, 2))
 F32 = jnp.float32
 BF16 = jnp.bfloat16
+CHUNKS = 4
+CHUNK_X = 16 // CHUNKS
+
+
+TOTAL = 80
 
 
 def packed_at(rows):
@@ -33,6 +38,7 @@
 
 LOW_AT, LOW_COUNT = packed_at(LOW_ROWS)
 HIGH_AT, HIGH_COUNT = packed_at(HIGH_ROWS)
+assert max(LOW_COUNT, HIGH_COUNT) <= TOTAL
 
 
 def plane_pieces(planes, total):
@@ -56,10 +62,8 @@
     return pieces
 
 
-LOW_TOTAL = 88
-HIGH_TOTAL = 80
-LOW_PIECES = plane_pieces(LOW_PLANES, LOW_TOTAL)
-HIGH_PIECES = plane_pieces(HIGH_PLANES, HIGH_TOTAL)
+LOW_PIECES = plane_pieces(LOW_PLANES, TOTAL)
+HIGH_PIECES = plane_pieces(HIGH_PLANES, TOTAL)
 
 
 def row_slice(first, count, step):
@@ -75,15 +79,37 @@
     return parts[0] + (parts[1] + parts[2])
 
 
-def prepare_kernel(block_ref, phase_ref, low_ref, high_ref, peak_ref):
+def phase_matrix(lanes, phases):
+    source = lax.broadcasted_iota(jnp.int32, (lanes, 128), 0)
+    target = lax.broadcasted_iota(jnp.int32, (lanes, 128), 1)
+    parts = [(source == 4 * target + p).astype(F32).astype(BF16) for p in phases]
+    return jnp.concatenate(parts, axis=1)
+
+
+def swap_by_parity(axis, first_ref, second_ref):
+    even = lax.rem(lax.axis_index(axis), 2) == 0
+    first, second = first_ref[...], second_ref[...]
+    return jnp.where(even, first, second), jnp.where(even, second, first)
+
+
+def prepare_kernel(block_hbm, raw_ref, near_ref, far_ref, peak_hbm, peak_ref, split_ref, low_ref, high_ref, sems):
+    copies = []
+    for c in range(2):
+        part = pl.ds(8 * c, 8)
+        copies.append(pltpu.make_async_copy(block_hbm.at[part], raw_ref.at[part], sems.at[c]))
+        copies[c].start()
+    matrix = phase_matrix(512, (0, 2))
+
     highest = [None] * 4
     lowest = [None] * 4
-    for x in range(16):
-        for t in range(2):
-            for k in range(4):
-                chunk = block_ref[x, 8 * t : 8 * t + 8, 128 * k : 128 * k + 128]
-                highest[k] = chunk if highest[k] is None else jnp.maximum(highest[k], chunk)
-                lowest[k] = chunk if lowest[k] is None else jnp.minimum(lowest[k], chunk)
+    for c in range(2):
+        copies[c].wait()
+        for x in range(8 * c, 8 * c + 8):
+            for t in range(2):
+                for k in range(4):
+                    chunk = raw_ref[x, 8 * t : 8 * t + 8, 128 * k : 128 * k + 128]
+                    highest[k] = chunk if highest[k] is None else jnp.maximum(highest[k], chunk)
+                    lowest[k] = chunk if lowest[k] is None else jnp.minimum(lowest[k], chunk)
     upper = jnp.maximum(jnp.maximum(highest[0], highest[1]), jnp.maximum(highest[2], highest[3]))
     lower = -jnp.minimum(jnp.minimum(lowest[0], lowest[1]), jnp.minimum(lowest[2], lowest[3]))
     lane = lax.broadcasted_iota(jnp.int32, (8, 128), 1)
@@ -94,11 +120,31 @@
         peak = jnp.maximum(peak, pltpu.roll(peak, s, 0))
     for i in range(peak_ref.shape[0] // 8):
         peak_ref[8 * i : 8 * i + 8, :] = peak
-
+    send = pltpu.make_async_copy(peak_ref, peak_hbm, sems.at[2])
+    send.start()
+
+    ys = sorted({y for _, y, _ in LOW_ROWS + HIGH_ROWS})
+    stacked = [
+        jnp.concatenate([raw_ref[8 * half : 8 * half + 8, y, 128 * k : 128 * k + 128] for k in range(4)], axis=1)
+        for y in ys
+        for half in range(2)
+    ]
+    split = permute_lanes(jnp.concatenate(stacked, axis=0), matrix)
+    for z in range(2):
+        split_ref[z] = split[:, 128 * z : 128 * z + 128]
+    for ref, rows, ats in ((low_ref, LOW_ROWS, LOW_AT), (high_ref, HIGH_ROWS, HIGH_AT)):
+        for (z, y, step), at in zip(rows, ats):
+            ref[at : at + 16 // step, :] = split_ref[z, row_slice(16 * ys.index(y), 16 // step, step), :]
+    low_ref[LOW_COUNT:TOTAL, :] = jnp.zeros((TOTAL - LOW_COUNT, 128), F32)
+    near_ref[...], far_ref[...] = swap_by_parity("gy", low_ref, high_ref)
+    send.wait()
+
+
+def split_kernel(raw_ref, phase_ref):
     source = lax.broadcasted_iota(jnp.int32, (256, 256), 0)
     target = lax.broadcasted_iota(jnp.int32, (256, 256), 1)
     matrix = (source == 4 * (target % 64) + target // 64).astype(F32).astype(BF16)
-    halves = [permute_lanes(block_ref[:, :, 256 * h : 256 * h + 256].reshape(256, 256), matrix) for h in range(2)]
+    halves = [permute_lanes(raw_ref[:, :, 256 * h : 256 * h + 256].reshape(256, 256), matrix) for h in range(2)]
     low_half = lax.broadcasted_iota(jnp.int32, (256, 128), 1) < 64
     for j in range(2):
         a = halves[0][:, 128 * j : 128 * j + 128]
@@ -106,15 +152,11 @@
         phase_ref[2 * j] = jnp.where(low_half, a, pltpu.roll(b, 64, 1))
         phase_ref[2 * j + 1] = jnp.where(low_half, pltpu.roll(a, 64, 1), b)
 
-    for ref, rows, places in ((low_ref, LOW_ROWS, LOW_AT), (high_ref, HIGH_ROWS, HIGH_AT)):
-        for (z, y, step), at in zip(rows, places):
-            for half in range(2 // step):
-                ref[at + 8 * half : at + 8 * half + 8, :] = phase_ref[
-                    2 * z, pl.ds(16 * 8 * half + y, 8, stride=16 * step), :
-                ]
-
-
-def join_kernel(phase_ref, ylow_ref, yhigh_ref, low_ref, high_ref, low_planes, high_planes):
+
+def join_kernel(
+    phase_ref, yfar_ref, ynear_ref, near_ref, far_ref, ylow_ref, yhigh_ref, low_ref, high_ref, low_planes, high_planes
+):
+    yhigh_ref[...], ylow_ref[...] = swap_by_parity("gy", ynear_ref, yfar_ref)
     for ref, planes, out, pieces in (
         (low_planes, LOW_PLANES, low_ref, LOW_PIECES),
         (high_planes, HIGH_PLANES, high_ref, HIGH_PIECES),
@@ -129,6 +171,20 @@
                         ref[r : r + 1, :] = source[at + x // step : at + x // step + 1, :]
         for i, z, x, first, count, step, at in pieces:
             out[at : at + count, :] = ref[row_slice(ROWS * i + first, count, step), :]
+    near_ref[...], far_ref[...] = swap_by_parity("gx", low_ref, high_ref)
+
+
+def merge_phases(parts, lane):
+    turned = [parts[0]] + [pltpu.roll(parts[p], 32 * p, 1) for p in (1, 2, 3)]
+    quarter = lane // 32
+    merged = []
+    for k in range(4):
+        block = turned[(3 - k) % 4]
+        for q in range(3):
+            block = jnp.where(quarter == q, turned[(q - k) % 4], block)
+        order = 32 * ((lane % 4 + k) % 4) + lane // 4
+        merged.append(jnp.take_along_axis(block, order, axis=1))
+    return merged
 
 
 def code_of(scaled):
@@ -142,8 +198,8 @@
 
 
 def compress_kernel(
-    phase_ref, ylow_ref, yhigh_ref, xlow_ref, xhigh_ref, peaks_ref, out_ref,
-    known0, known2, codes0, codes2, full0, full2, fullc0, fullc1, fullc2, fullc3,
+    phase_ref, ylow_ref, yhigh_ref, xnear_ref, xfar_ref, peaks_ref, out_hbm,
+    known0, known2, codes0, codes2, full0, full2, fullc0, fullc2, xlow_ref, xhigh_ref, out_ref, sems,
 ):
     lane = lax.broadcasted_iota(jnp.int32, (8, 128), 1)
     known = (known0, known2)
@@ -154,6 +210,7 @@
     def plane(x):
         return (x + OWN_X) * ROWS
 
+    xhigh_ref[...], xlow_ref[...] = swap_by_parity("gx", xnear_ref, xfar_ref)
     for z in range(2):
         for x in range(16):
             base = plane(x) + OWN_R
@@ -218,7 +275,7 @@
                 known[z][pl.ds(plane(x) + first, count), :] = value
                 codes[z][pl.ds(plane(x) + first, count), :] = code
 
-    for x in range(16):
+    def last_steps(x):
         for z in range(2):
             base = plane(x) + OWN_R
             inner = known[z][pl.ds(base, 8), :]
@@ -240,75 +297,95 @@
             k0_next = pltpu.roll(k0, 127, 1)
             k2_next = pltpu.roll(k2, 127, 1)
             k2_last = pltpu.roll(k2, 1, 1)
-            fullc1[rows, :], _ = quantize(phase_ref[1, rows, :], k2_last, k0, k2, k0_next)
-            fullc3[rows, :], _ = quantize(phase_ref[3, rows, :], k0, k2, k0_next, k2_next)
-
-    source = lax.broadcasted_iota(jnp.int32, (256, 256), 0)
-    target = lax.broadcasted_iota(jnp.int32, (256, 256), 1)
-    matrix = (target == 4 * (source % 64) + source // 64).astype(F32).astype(BF16)
-    low_half = lax.broadcasted_iota(jnp.int32, (256, 128), 1) < 64
-    parts = [fullc0[...], fullc1[...], fullc2[...], fullc3[...]]
-    turned = [pltpu.roll(p, 64, 1) for p in parts]
-    first = jnp.concatenate(
-        [jnp.where(low_half, parts[0], turned[1]), jnp.where(low_half, parts[2], turned[3])], axis=1
-    )
-    second = jnp.concatenate(
-        [jnp.where(low_half, turned[0], parts[1]), jnp.where(low_half, turned[2], parts[3])], axis=1
-    )
-    out_ref[:, :, 0:256] = permute_lanes(first, matrix).reshape(16, 16, 256)
-    out_ref[:, :, 256:512] = permute_lanes(second, matrix).reshape(16, 16, 256)
+            code1, _ = quantize(phase_ref[1, rows, :], k2_last, k0, k2, k0_next)
+            code3, _ = quantize(phase_ref[3, rows, :], k0, k2, k0_next, k2_next)
+            merged = merge_phases([fullc0[rows, :], code1, fullc2[rows, :], code3], lane)
+            for k in range(4):
+                out_ref[x, 8 * t : 8 * t + 8, 128 * k : 128 * k + 128] = merged[k]
+
+    copies = []
+    for c in range(CHUNKS):
+        for x in range(c * CHUNK_X, c * CHUNK_X + CHUNK_X):
+            last_steps(x)
+        part = pl.ds(c * CHUNK_X, CHUNK_X)
+        copies.append(pltpu.make_async_copy(out_ref.at[part], out_hbm.at[part], sems.at[c]))
+        copies[c].start()
+    for copy in copies:
+        copy.wait()
 
 
 def shards(snapshot):
     nx = lax.axis_size("gx")
     ny = lax.axis_size("gy")
     vmem = pl.BlockSpec(memory_space=pltpu.VMEM)
+    hbm = pl.BlockSpec(memory_space=pltpu.HBM)
     block = snapshot.reshape(snapshot.shape[1:])
     params = pltpu.CompilerParams(vmem_limit_bytes=16 * 1024 * 1024)
 
     def shape(*dims):
         return jax.ShapeDtypeStruct(dims, F32)
 
-    phases, low, high, peak = pl.pallas_call(
+    block = pltpu.with_memory_space_constraint(block, pltpu.HBM)
+    raw, near, far, peak = pl.pallas_call(
         prepare_kernel,
-        in_specs=[vmem],
-        out_specs=[vmem] * 4,
-        out_shape=[shape(4, 256, 128), shape(LOW_COUNT, 128), shape(HIGH_COUNT, 128), shape(nx * ny, 128)],
+        in_specs=[hbm],
+        out_specs=[vmem] * 3 + [hbm],
+        out_shape=[shape(*block.shape), shape(TOTAL, 128), shape(TOTAL, 128), shape(nx * ny, 128)],
+        scratch_shapes=[
+            pltpu.VMEM((nx * ny, 128), F32),
+            pltpu.VMEM((2, 16 * 6, 128), F32),
+            pltpu.VMEM((TOTAL, 128), F32),
+            pltpu.VMEM((TOTAL, 128), F32),
+            pltpu.SemaphoreType.DMA((3,)),
+        ],
         compiler_params=params,
         name="prepare",
     )(block)
-
-    def shifted(array, axis, d):
+    phases = pl.pallas_call(
+        split_kernel,
+        in_specs=[vmem],
+        out_specs=vmem,
+        out_shape=shape(4, 256, 128),
+        compiler_params=params,
+        name="split",
+    )(raw)
+
+    def exchanged(array, axis, odd):
         n = lax.axis_size(axis)
-        return lax.ppermute(array, axis, [(i, (i + d) % n) for i in range(n)])
+        return lax.ppermute(array, axis, [(i, (i + (1 if i % 2 == odd else -1)) % n) for i in range(n)])
 
     peaks = lax.all_to_all(peak, AXES, 0, 0, tiled=True)
-    ylow = shifted(low, "gy", 1)
-    yhigh = shifted(high, "gy", -1)
-    low_planes, high_planes = pl.pallas_call(
+    yfar = exchanged(far, "gy", 1)
+    ynear = exchanged(near, "gy", 0)
+    near, far, ylow, yhigh = pl.pallas_call(
         join_kernel,
         in_specs=[vmem] * 3,
-        out_specs=[vmem] * 2,
-        out_shape=[shape(LOW_TOTAL, 128), shape(HIGH_TOTAL, 128)],
+        out_specs=[vmem] * 4,
+        out_shape=[shape(TOTAL, 128)] * 4,
         scratch_shapes=[
+            pltpu.VMEM((TOTAL, 128), F32),
+            pltpu.VMEM((TOTAL, 128), F32),
             pltpu.VMEM((ROWS * len(LOW_PLANES), 128), F32),
             pltpu.VMEM((ROWS * len(HIGH_PLANES), 128), F32),
         ],
         compiler_params=params,
         name="join",
-    )(phases, ylow, yhigh)
-    xlow = shifted(low_planes, "gx", 1)
-    xhigh = shifted(high_planes, "gx", -1)
+    )(phases, yfar, ynear)
+    xnear = exchanged(near, "gx", 0)
+    xfar = exchanged(far, "gx", 1)
 
     codes = pl.pallas_call(
         compress_kernel,
         in_specs=[vmem] * 6,
-        out_specs=vmem,
+        out_specs=hbm,
         out_shape=shape(*block.shape),
-        scratch_shapes=[pltpu.VMEM((PLANES * ROWS, 128), F32)] * 4 + [pltpu.VMEM((256, 128), F32)] * 6,
+        scratch_shapes=[pltpu.VMEM((PLANES * ROWS, 128), F32)] * 4
+        + [pltpu.VMEM((256, 128), F32)] * 4
+        + [pltpu.VMEM((TOTAL, 128), F32)] * 2
+        + [pltpu.VMEM(block.shape, F32), pltpu.SemaphoreType.DMA((CHUNKS,))],
         compiler_params=params,
         name="compress",
-    )(phases, ylow, yhigh, xlow, xhigh, peaks)
+    )(phases, ylow, yhigh, xnear, xfar, peaks)
     return codes.reshape(snapshot.shape)
 
 

time: 33.4 us -> 32.8 us (0.982)
  the two profiles are of different devices: /device:TPU:96 before, /device:TPU:1 now
where the time goes in v4:
time: 32.8 us; the launch traced here: 32.5 us
  starting transfers between devices  26.4 us (80%)
  Pallas kernels  4.36 us (13%)
  waiting for transfers between devices  1.74 us (5%)
    all_to_all x1, starting transfers between devices, shards(): peaks = lax.all_to_all(peak, AXES, 0, 0, tiled=True)  15.7 us
    ppermute x4, starting transfers between devices, exchanged(): lax.ppermute(array, axis, [(i, (i + (1 if i % 2 == odd else -1)) % n) for...  10.7 us
    pallas_call x1, Pallas kernels, shards(): pl.pallas_call(prepare_kernel, in_specs=[hbm], out_specs=[vmem] * 3 + [hb...  1.96 us
    pallas_call x1, Pallas kernels, shards(): pl.pallas_call(compress_kernel, in_specs=[vmem] * 6, out_specs=hbm, out_s...  1.82 us
    ppermute x4, waiting for transfers between devices, exchanged(): lax.ppermute(array, axis, [(i, (i + (1 if i % 2 == odd else -1)) % n) for...  1.74 us
  transfers between devices with their start and end apart: 5, of which 3 were waited for; matrix products, arithmetic and copies ran while one was open for 0% of the time, Pallas kernels for 2%

profile of v4, /device:TPU:1, one launch (start us, length us, event | category | flops | bytes accessed | tf_op | source)
XLA Modules:
  0.0 32.5 jit_solution(7158143357109810114)
XLA Ops:
  0.0 2.0 %prepare.1 = (f32[16,16,512]{2,1,0:T(8,128)S(1)}, f32[80,128]{1,0:T(8,128)S(1)}, f32[80,128]{1,0:T(8,128)S(1)}, f32[256,128]{1,0:T(8,128)}) custom-call(f32[16,16,512]{2,1,0:T(8,128)} %bitcast.7), custom_call_target="tpu_custom_call" | custom-call | tf_op jit(solution)/shard_map/prepare/pallas_call | solution.py:329
  2.0 15.7 %all-to-all-start = ((f32[256,1,128]{2,1,0:T(1,128)}), f32[256,1,128]{2,1,0:T(1,128)S(1)}, u32[]{:S(2)}, u32[]{:S(2)}) async-start(f32[256,1,128]{2,1,0:T(1,128)} %bitcast.2), calls=%async_computation | async-start | bytes 262144 | tf_op jit(solution)/shard_map/all_to_all | solution.py:357
  17.6 1.7 %collective-permute-start = (f32[80,128]{1,0:T(8,128)S(1)}, f32[80,128]{1,0:T(8,128)S(1)}, u32[]{:S(2)}, u32[]{:S(2)}) collective-permute-start(f32[80,128]{1,0:T(8,128)S(1)} %get-tuple-element.14), channel_id=1, source_target_pairs={{0,7},{1,2},{2,1},{3,4},{4,3},{5,6},{6,5},{7,0},{8,15},{9,10},{10,... | collective-permute-start | bytes 122888 | tf_op jit(solution)/shard_map/ppermute | solution.py:355
  19.4 1.4 %collective-permute-start.1 = (f32[80,128]{1,0:T(8,128)S(1)}, f32[80,128]{1,0:T(8,128)S(1)}, u32[]{:S(2)}, u32[]{:S(2)}) collective-permute-start(f32[80,128]{1,0:T(8,128)S(1)} %get-tuple-element.15), channel_id=1, source_target_pairs={{0,1},{1,0},{2,3},{3,2},{4,5},{5,4},{6,7},{7,6},{8,9},{9,8},{10,11... | collective-permute-start | bytes 122888 | tf_op jit(solution)/shard_map/ppermute | solution.py:355
  20.7 0.5 %split.1.phase_ref = f32[4,256,128]{2,1,0:T(8,128)S(1)} custom-call(f32[16,16,512]{2,1,0:T(8,128)S(1)} %get-tuple-element.13.raw_ref), custom_call_target="tpu_custom_call" | custom-call | tf_op jit(solution)/shard_map/split/pallas_call | solution.py:344
  21.3 0.3 collective-permute-done.yfar_ref
  21.5 0.1 collective-permute-done.1.ynear_ref
  21.6 0.1 join.1
  21.7 1.6 %collective-permute-start.2 = (f32[80,128]{1,0:T(8,128)S(1)}, f32[80,128]{1,0:T(8,128)S(1)}, u32[]{:S(2)}, u32[]{:S(2)}) collective-permute-start(f32[80,128]{1,0:T(8,128)S(1)} %get-tuple-element.18), channel_id=1, source_target_pairs={{0,8},{8,0},{16,24},{24,16},{32,40},{40,32},{48,56},{56,48},{64,72... | collective-permute-start | bytes 122888 | tf_op jit(solution)/shard_map/ppermute | solution.py:355
  23.2 6.1 %collective-permute-start.3 = (f32[80,128]{1,0:T(8,128)S(1)}, f32[80,128]{1,0:T(8,128)S(1)}, u32[]{:S(2)}, u32[]{:S(2)}) collective-permute-start(f32[80,128]{1,0:T(8,128)S(1)} %get-tuple-element.19), channel_id=1, source_target_pairs={{0,248},{8,16},{16,8},{24,32},{32,24},{40,48},{48,40},{56,64},{64,... | collective-permute-start | bytes 122888 | tf_op jit(solution)/shard_map/ppermute | solution.py:355
  29.3 0.0 collective-permute-done.2.xnear_ref
  29.3 1.4 %collective-permute-done.3.xfar_ref = f32[80,128]{1,0:T(8,128)S(1)} collective-permute-done((f32[80,128]{1,0:T(8,128)S(1)}, f32[80,128]{1,0:T(8,128)S(1)}, u32[]{:S(2)}, u32[]{:S(2)}) %collective-permute-start.3) | collective-permute-done | bytes 40992 | tf_op jit(solution)/shard_map/ppermute | solution.py:355
  30.7 0.0 all-to-all-done
  30.7 1.8 %compress.1 = f32[16,16,512]{2,1,0:T(8,128)} custom-call(f32[4,256,128]{2,1,0:T(8,128)S(1)} %split.1.phase_ref, f32[80,128]{1,0:T(8,128)S(1)} %get-tuple-element.16.ylow_ref, f32[80,128]{1,0:T(8,128)S(1)} %get-tuple-element.17.yhigh_ref, f32[80,128]{1,0:T(8,128)S(1)} %collective-permute-done.2.xnear_ref, f32[80,128]{1,0:T(8,128)S(1)} %collective-permute-done.3.xfar_ref, ...), custom_call_target="tpu_custom_call" | custom-call | tf_op jit(solution)/shard_map/compress/pallas_call | solution.py:377
Async XLA Ops:
  2.0 28.7 %all-to-all-start = ((f32[256,1,128]{2,1,0:T(1,128)}), f32[256,1,128]{2,1,0:T(1,128)S(1)}, u32[]{:S(2)}, u32[]{:S(2)}) async-start(f32[256,1,128]{2,1,0:T(1,128)} %bitcast.2), calls=%async_computation | async-start | bytes 262144 | tf_op jit(solution)/shard_map/all_to_all | solution.py:357
  17.6 3.9 %collective-permute-start = (f32[80,128]{1,0:T(8,128)S(1)}, f32[80,128]{1,0:T(8,128)S(1)}, u32[]{:S(2)}, u32[]{:S(2)}) collective-permute-start(f32[80,128]{1,0:T(8,128)S(1)} %get-tuple-element.14), channel_id=1, source_target_pairs={{0,7},{1,2},{2,1},{3,4},{4,3},{5,6},{6,5},{7,0},{8,15},{9,10},{10,... | collective-permute-start | bytes 122888 | tf_op jit(solution)/shard_map/ppermute | solution.py:355
  19.4 2.2 %collective-permute-start.1 = (f32[80,128]{1,0:T(8,128)S(1)}, f32[80,128]{1,0:T(8,128)S(1)}, u32[]{:S(2)}, u32[]{:S(2)}) collective-permute-start(f32[80,128]{1,0:T(8,128)S(1)} %get-tuple-element.15), channel_id=1, source_target_pairs={{0,1},{1,0},{2,3},{3,2},{4,5},{5,4},{6,7},{7,6},{8,9},{9,8},{10,11... | collective-permute-start | bytes 122888 | tf_op jit(solution)/shard_map/ppermute | solution.py:355
  21.7 7.7 %collective-permute-start.2 = (f32[80,128]{1,0:T(8,128)S(1)}, f32[80,128]{1,0:T(8,128)S(1)}, u32[]{:S(2)}, u32[]{:S(2)}) collective-permute-start(f32[80,128]{1,0:T(8,128)S(1)} %get-tuple-element.18), channel_id=1, source_target_pairs={{0,8},{8,0},{16,24},{24,16},{32,40},{40,32},{48,56},{56,48},{64,72... | collective-permute-start | bytes 122888 | tf_op jit(solution)/shard_map/ppermute | solution.py:355
  23.2 7.5 %collective-permute-start.3 = (f32[80,128]{1,0:T(8,128)S(1)}, f32[80,128]{1,0:T(8,128)S(1)}, u32[]{:S(2)}, u32[]{:S(2)}) collective-permute-start(f32[80,128]{1,0:T(8,128)S(1)} %get-tuple-element.19), channel_id=1, source_target_pairs={{0,248},{8,16},{16,8},{24,32},{32,24},{40,48},{48,40},{56,64},{64,... | collective-permute-start | bytes 122888 | tf_op jit(solution)/shard_map/ppermute | solution.py:355

commit v5 on v4

--- a/solution.py
+++ b/solution.py
@@ -154,7 +154,7 @@
 
 
 def join_kernel(
-    phase_ref, yfar_ref, ynear_ref, near_ref, far_ref, ylow_ref, yhigh_ref, low_ref, high_ref, low_planes, high_planes
+    phase_ref, yfar_ref, ynear_ref, low_ref, high_ref, ylow_ref, yhigh_ref, low_planes, high_planes
 ):
     yhigh_ref[...], ylow_ref[...] = swap_by_parity("gy", ynear_ref, yfar_ref)
     for ref, planes, out, pieces in (
@@ -171,7 +171,6 @@
                         ref[r : r + 1, :] = source[at + x // step : at + x // step + 1, :]
         for i, z, x, first, count, step, at in pieces:
             out[at : at + count, :] = ref[row_slice(ROWS * i + first, count, step), :]
-    near_ref[...], far_ref[...] = swap_by_parity("gx", low_ref, high_ref)
 
 
 def merge_phases(parts, lane):
@@ -198,8 +197,8 @@
 
 
 def compress_kernel(
-    phase_ref, ylow_ref, yhigh_ref, xnear_ref, xfar_ref, peaks_ref, out_hbm,
-    known0, known2, codes0, codes2, full0, full2, fullc0, fullc2, xlow_ref, xhigh_ref, out_ref, sems,
+    phase_ref, ylow_ref, yhigh_ref, xlow_ref, xhigh_ref, peaks_ref, out_hbm,
+    known0, known2, codes0, codes2, full0, full2, fullc0, fullc2, out_ref, sems,
 ):
     lane = lax.broadcasted_iota(jnp.int32, (8, 128), 1)
     known = (known0, known2)
@@ -210,7 +209,6 @@
     def plane(x):
         return (x + OWN_X) * ROWS
 
-    xhigh_ref[...], xlow_ref[...] = swap_by_parity("gx", xnear_ref, xfar_ref)
     for z in range(2):
         for x in range(16):
             base = plane(x) + OWN_R
@@ -350,6 +348,10 @@
         name="split",
     )(raw)
 
+    def shifted(array, axis, d):
+        n = lax.axis_size(axis)
+        return lax.ppermute(array, axis, [(i, (i + d) % n) for i in range(n)])
+
     def exchanged(array, axis, odd):
         n = lax.axis_size(axis)
         return lax.ppermute(array, axis, [(i, (i + (1 if i % 2 == odd else -1)) % n) for i in range(n)])
@@ -357,22 +359,20 @@
     peaks = lax.all_to_all(peak, AXES, 0, 0, tiled=True)
     yfar = exchanged(far, "gy", 1)
     ynear = exchanged(near, "gy", 0)
-    near, far, ylow, yhigh = pl.pallas_call(
+    low, high, ylow, yhigh = pl.pallas_call(
         join_kernel,
         in_specs=[vmem] * 3,
         out_specs=[vmem] * 4,
         out_shape=[shape(TOTAL, 128)] * 4,
         scratch_shapes=[
-            pltpu.VMEM((TOTAL, 128), F32),
-            pltpu.VMEM((TOTAL, 128), F32),
             pltpu.VMEM((ROWS * len(LOW_PLANES), 128), F32),
             pltpu.VMEM((ROWS * len(HIGH_PLANES), 128), F32),
         ],
         compiler_params=params,
         name="join",
     )(phases, yfar, ynear)
-    xnear = exchanged(near, "gx", 0)
-    xfar = exchanged(far, "gx", 1)
+    xlow = shifted(low, "gx", 1)
+    xhigh = shifted(high, "gx", -1)
 
     codes = pl.pallas_call(
         compress_kernel,
@@ -381,11 +381,10 @@
         out_shape=shape(*block.shape),
         scratch_shapes=[pltpu.VMEM((PLANES * ROWS, 128), F32)] * 4
         + [pltpu.VMEM((256, 128), F32)] * 4
-        + [pltpu.VMEM((TOTAL, 128), F32)] * 2
         + [pltpu.VMEM(block.shape, F32), pltpu.SemaphoreType.DMA((CHUNKS,))],
         compiler_params=params,
         name="compress",
-    )(phases, ylow, yhigh, xnear, xfar, peaks)
+    )(phases, ylow, yhigh, xlow, xhigh, peaks)
     return codes.reshape(snapshot.shape)
 
 

time: 32.8 us -> 32.3 us (0.985)
  starting transfers between devices: 26.4 us -> 25.6 us
  waiting for transfers between devices: 1.74 us -> 2.24 us
    ppermute x4 -> x2, starting transfers between devices: 10.7 us -> 3.08 us  [exchanged(): lax.ppermute(array, axis, [(i, (i + (1 if i % 2 == odd else -1)) % n) for...]
    ppermute x0 -> x2, starting transfers between devices: none -> 6.83 us  [shifted(): return lax.ppermute(array, axis, [(i, (i + d) % n) for i in range(n)])]
    ppermute x0 -> x2, waiting for transfers between devices: none -> 1.6 us  [shifted(): return lax.ppermute(array, axis, [(i, (i + d) % n) for i in range(n)])]
    ppermute x4 -> x2, waiting for transfers between devices: 1.74 us -> 0.34 us  [exchanged(): lax.ppermute(array, axis, [(i, (i + (1 if i % 2 == odd else -1)) % n) for...]
  transfers between devices with their start and end apart: 5 -> 5, of which waited for: 3 -> 4; matrix products, arithmetic and copies ran while one was open for 0% -> 0% of each run, Pallas kernels for 2% -> 2%
where the time goes in v5:
time: 32.3 us; the launch traced here: 32.2 us
  starting transfers between devices  25.6 us (79%)
  Pallas kernels  4.36 us (13%)
  waiting for transfers between devices  2.24 us (7%)
    all_to_all x1, starting transfers between devices, shards(): peaks = lax.all_to_all(peak, AXES, 0, 0, tiled=True)  15.7 us
    ppermute x2, starting transfers between devices, shifted(): return lax.ppermute(array, axis, [(i, (i + d) % n) for i in range(n)])  6.83 us
    ppermute x2, starting transfers between devices, exchanged(): lax.ppermute(array, axis, [(i, (i + (1 if i % 2 == odd else -1)) % n) for...  3.08 us
    pallas_call x1, Pallas kernels, shards(): pl.pallas_call(prepare_kernel, in_specs=[hbm], out_specs=[vmem] * 3 + [hb...  1.96 us
    pallas_call x1, Pallas kernels, shards(): pl.pallas_call(compress_kernel, in_specs=[vmem] * 6, out_specs=hbm, out_s...  1.82 us
    ppermute x2, waiting for transfers between devices, shifted(): return lax.ppermute(array, axis, [(i, (i + d) % n) for i in range(n)])  1.6 us
  transfers between devices with their start and end apart: 5, of which 4 were waited for; matrix products, arithmetic and copies ran while one was open for 0% of the time, Pallas kernels for 2%

profile of v5, /device:TPU:1, one launch (start us, length us, event | category | flops | bytes accessed | tf_op | source)
XLA Modules:
  0.0 32.2 jit_solution(5973197427967584756)
XLA Ops:
  0.0 2.0 %prepare.1 = (f32[16,16,512]{2,1,0:T(8,128)S(1)}, f32[80,128]{1,0:T(8,128)S(1)}, f32[80,128]{1,0:T(8,128)S(1)}, f32[256,128]{1,0:T(8,128)}) custom-call(f32[16,16,512]{2,1,0:T(8,128)} %bitcast.7), custom_call_target="tpu_custom_call" | custom-call | tf_op jit(solution)/shard_map/prepare/pallas_call | solution.py:327
  2.0 15.7 %all-to-all-start = ((f32[256,1,128]{2,1,0:T(1,128)}), f32[256,1,128]{2,1,0:T(1,128)S(1)}, u32[]{:S(2)}, u32[]{:S(2)}) async-start(f32[256,1,128]{2,1,0:T(1,128)} %bitcast.2), calls=%async_computation | async-start | bytes 262144 | tf_op jit(solution)/shard_map/all_to_all | solution.py:359
  17.6 1.7 %collective-permute-start = (f32[80,128]{1,0:T(8,128)S(1)}, f32[80,128]{1,0:T(8,128)S(1)}, u32[]{:S(2)}, u32[]{:S(2)}) collective-permute-start(f32[80,128]{1,0:T(8,128)S(1)} %get-tuple-element.14), channel_id=1, source_target_pairs={{0,7},{1,2},{2,1},{3,4},{4,3},{5,6},{6,5},{7,0},{8,15},{9,10},{10,... | collective-permute-start | bytes 122888 | tf_op jit(solution)/shard_map/ppermute | solution.py:357
  19.4 1.4 %collective-permute-start.1 = (f32[80,128]{1,0:T(8,128)S(1)}, f32[80,128]{1,0:T(8,128)S(1)}, u32[]{:S(2)}, u32[]{:S(2)}) collective-permute-start(f32[80,128]{1,0:T(8,128)S(1)} %get-tuple-element.15), channel_id=1, source_target_pairs={{0,1},{1,0},{2,3},{3,2},{4,5},{5,4},{6,7},{7,6},{8,9},{9,8},{10,11... | collective-permute-start | bytes 122888 | tf_op jit(solution)/shard_map/ppermute | solution.py:357
  20.7 0.5 %split.1.phase_ref = f32[4,256,128]{2,1,0:T(8,128)S(1)} custom-call(f32[16,16,512]{2,1,0:T(8,128)S(1)} %get-tuple-element.13.raw_ref), custom_call_target="tpu_custom_call" | custom-call | tf_op jit(solution)/shard_map/split/pallas_call | solution.py:342
  21.3 0.3 collective-permute-done.yfar_ref
  21.5 0.1 collective-permute-done.1.ynear_ref
  21.6 1.5 %collective-permute-start.2 = (f32[80,128]{1,0:T(8,128)S(1)}, f32[80,128]{1,0:T(8,128)S(1)}, u32[]{:S(2)}, u32[]{:S(2)}) collective-permute-start(f32[80,128]{1,0:T(8,128)S(1)} %get-tuple-element.18), channel_id=1, source_target_pairs={{0,8},{8,16},{16,24},{24,32},{32,40},{40,48},{48,56},{56,64},{64,7... | collective-permute-start | bytes 122888 | tf_op jit(solution)/shard_map/ppermute | solution.py:353
  23.2 5.3 %collective-permute-start.3 = (f32[80,128]{1,0:T(8,128)S(1)}, f32[80,128]{1,0:T(8,128)S(1)}, u32[]{:S(2)}, u32[]{:S(2)}) collective-permute-start(f32[80,128]{1,0:T(8,128)S(1)} %get-tuple-element.19), channel_id=1, source_target_pairs={{0,248},{8,0},{16,8},{24,16},{32,24},{40,32},{48,40},{56,48},{64,5... | collective-permute-start | bytes 122888 | tf_op jit(solution)/shard_map/ppermute | solution.py:353
  28.5 1.6 %collective-permute-done.2.xlow_ref = f32[80,128]{1,0:T(8,128)S(1)} collective-permute-done((f32[80,128]{1,0:T(8,128)S(1)}, f32[80,128]{1,0:T(8,128)S(1)}, u32[]{:S(2)}, u32[]{:S(2)}) %collective-permute-start.2) | collective-permute-done | bytes 40992 | tf_op jit(solution)/shard_map/ppermute | solution.py:353
  30.1 0.0 collective-permute-done.3.xhigh_ref
  30.1 0.3 all-to-all-done
  30.4 1.8 %compress.1 = f32[16,16,512]{2,1,0:T(8,128)} custom-call(f32[4,256,128]{2,1,0:T(8,128)S(1)} %split.1.phase_ref, f32[80,128]{1,0:T(8,128)S(1)} %get-tuple-element.16.ylow_ref, f32[80,128]{1,0:T(8,128)S(1)} %get-tuple-element.17.yhigh_ref, f32[80,128]{1,0:T(8,128)S(1)} %collective-permute-done.2.xlow_ref, f32[80,128]{1,0:T(8,128)S(1)} %collective-permute-done.3.xhigh_ref, ...), custom_call_target="tpu_custom_call" | custom-call | tf_op jit(solution)/shard_map/compress/pallas_call | solution.py:377
  (1 shorter events, 0.0 us)
Async XLA Ops:
  2.0 28.4 %all-to-all-start = ((f32[256,1,128]{2,1,0:T(1,128)}), f32[256,1,128]{2,1,0:T(1,128)S(1)}, u32[]{:S(2)}, u32[]{:S(2)}) async-start(f32[256,1,128]{2,1,0:T(1,128)} %bitcast.2), calls=%async_computation | async-start | bytes 262144 | tf_op jit(solution)/shard_map/all_to_all | solution.py:359
  17.6 3.9 %collective-permute-start = (f32[80,128]{1,0:T(8,128)S(1)}, f32[80,128]{1,0:T(8,128)S(1)}, u32[]{:S(2)}, u32[]{:S(2)}) collective-permute-start(f32[80,128]{1,0:T(8,128)S(1)} %get-tuple-element.14), channel_id=1, source_target_pairs={{0,7},{1,2},{2,1},{3,4},{4,3},{5,6},{6,5},{7,0},{8,15},{9,10},{10,... | collective-permute-start | bytes 122888 | tf_op jit(solution)/shard_map/ppermute | solution.py:357
  19.4 2.2 %collective-permute-start.1 = (f32[80,128]{1,0:T(8,128)S(1)}, f32[80,128]{1,0:T(8,128)S(1)}, u32[]{:S(2)}, u32[]{:S(2)}) collective-permute-start(f32[80,128]{1,0:T(8,128)S(1)} %get-tuple-element.15), channel_id=1, source_target_pairs={{0,1},{1,0},{2,3},{3,2},{4,5},{5,4},{6,7},{7,6},{8,9},{9,8},{10,11... | collective-permute-start | bytes 122888 | tf_op jit(solution)/shard_map/ppermute | solution.py:357
  21.6 8.4 %collective-permute-start.2 = (f32[80,128]{1,0:T(8,128)S(1)}, f32[80,128]{1,0:T(8,128)S(1)}, u32[]{:S(2)}, u32[]{:S(2)}) collective-permute-start(f32[80,128]{1,0:T(8,128)S(1)} %get-tuple-element.18), channel_id=1, source_target_pairs={{0,8},{8,16},{16,24},{24,32},{32,40},{40,48},{48,56},{56,64},{64,7... | collective-permute-start | bytes 122888 | tf_op jit(solution)/shard_map/ppermute | solution.py:353
  23.2 6.9 %collective-permute-start.3 = (f32[80,128]{1,0:T(8,128)S(1)}, f32[80,128]{1,0:T(8,128)S(1)}, u32[]{:S(2)}, u32[]{:S(2)}) collective-permute-start(f32[80,128]{1,0:T(8,128)S(1)} %get-tuple-element.19), channel_id=1, source_target_pairs={{0,248},{8,0},{16,8},{24,16},{32,24},{40,32},{48,40},{56,48},{64,5... | collective-permute-start | bytes 122888 | tf_op jit(solution)/shard_map/ppermute | solution.py:353

commit v6 on v5

--- a/solution.py
+++ b/solution.py
@@ -92,13 +92,12 @@
     return jnp.where(even, first, second), jnp.where(even, second, first)
 
 
-def prepare_kernel(block_hbm, raw_ref, near_ref, far_ref, peak_hbm, peak_ref, split_ref, low_ref, high_ref, sems):
+def prepare_kernel(block_hbm, raw_ref, peak_hbm, peak_ref, sems):
     copies = []
     for c in range(2):
         part = pl.ds(8 * c, 8)
         copies.append(pltpu.make_async_copy(block_hbm.at[part], raw_ref.at[part], sems.at[c]))
         copies[c].start()
-    matrix = phase_matrix(512, (0, 2))
 
     highest = [None] * 4
     lowest = [None] * 4
@@ -123,6 +122,11 @@
     send = pltpu.make_async_copy(peak_ref, peak_hbm, sems.at[2])
     send.start()
 
+    send.wait()
+
+
+def rows_kernel(raw_ref, near_ref, far_ref, split_ref, low_ref, high_ref):
+    matrix = phase_matrix(512, (0, 2))
     ys = sorted({y for _, y, _ in LOW_ROWS + HIGH_ROWS})
     stacked = [
         jnp.concatenate([raw_ref[8 * half : 8 * half + 8, y, 128 * k : 128 * k + 128] for k in range(4)], axis=1)
@@ -137,7 +141,6 @@
             ref[at : at + 16 // step, :] = split_ref[z, row_slice(16 * ys.index(y), 16 // step, step), :]
     low_ref[LOW_COUNT:TOTAL, :] = jnp.zeros((TOTAL - LOW_COUNT, 128), F32)
     near_ref[...], far_ref[...] = swap_by_parity("gy", low_ref, high_ref)
-    send.wait()
 
 
 def split_kernel(raw_ref, phase_ref):
@@ -324,21 +327,28 @@
         return jax.ShapeDtypeStruct(dims, F32)
 
     block = pltpu.with_memory_space_constraint(block, pltpu.HBM)
-    raw, near, far, peak = pl.pallas_call(
+    raw, peak = pl.pallas_call(
         prepare_kernel,
         in_specs=[hbm],
-        out_specs=[vmem] * 3 + [hbm],
-        out_shape=[shape(*block.shape), shape(TOTAL, 128), shape(TOTAL, 128), shape(nx * ny, 128)],
+        out_specs=[vmem, hbm],
+        out_shape=[shape(*block.shape), shape(nx * ny, 128)],
+        scratch_shapes=[pltpu.VMEM((nx * ny, 128), F32), pltpu.SemaphoreType.DMA((3,))],
+        compiler_params=params,
+        name="prepare",
+    )(block)
+    near, far = pl.pallas_call(
+        rows_kernel,
+        in_specs=[vmem],
+        out_specs=[vmem] * 2,
+        out_shape=[shape(TOTAL, 128)] * 2,
         scratch_shapes=[
-            pltpu.VMEM((nx * ny, 128), F32),
             pltpu.VMEM((2, 16 * 6, 128), F32),
             pltpu.VMEM((TOTAL, 128), F32),
             pltpu.VMEM((TOTAL, 128), F32),
-            pltpu.SemaphoreType.DMA((3,)),
         ],
         compiler_params=params,
-        name="prepare",
-    )(block)
+        name="rows",
+    )(raw)
     phases = pl.pallas_call(
         split_kernel,
         in_specs=[vmem],

time: 32.3 us -> 32.2 us (level)
    pallas_call x1 -> x2, Pallas kernels: 1.96 us -> 2.17 us  [the longest x1 1.81 us: shards(): pl.pallas_call(prepare_kernel, in_specs=[hbm], out_specs=[vmem, hbm], out...]
  transfers between devices with their start and end apart: 5 -> 5, of which waited for: 4 -> 3; matrix products, arithmetic and copies ran while one was open for 0% -> 0% of each run, Pallas kernels for 2% -> 3%
where the time goes in v6:
time: 32.2 us; the launch traced here: 32.1 us
  starting transfers between devices  25.6 us (80%)
  Pallas kernels  4.56 us (14%)
  waiting for transfers between devices  1.94 us (6%)
    all_to_all x1, starting transfers between devices, shards(): peaks = lax.all_to_all(peak, AXES, 0, 0, tiled=True)  15.7 us
    ppermute x2, starting transfers between devices, shifted(): return lax.ppermute(array, axis, [(i, (i + d) % n) for i in range(n)])  6.81 us
    ppermute x2, starting transfers between devices, exchanged(): lax.ppermute(array, axis, [(i, (i + (1 if i % 2 == odd else -1)) % n) for...  3.08 us
    pallas_call x1, Pallas kernels, shards(): pl.pallas_call(compress_kernel, in_specs=[vmem] * 6, out_specs=hbm, out_s...  1.82 us
    pallas_call x1, Pallas kernels, shards(): pl.pallas_call(prepare_kernel, in_specs=[hbm], out_specs=[vmem, hbm], out...  1.81 us
    ppermute x2, waiting for transfers between devices, shifted(): return lax.ppermute(array, axis, [(i, (i + d) % n) for i in range(n)])  1.6 us
  transfers between devices with their start and end apart: 5, of which 3 were waited for; matrix products, arithmetic and copies ran while one was open for 0% of the time, Pallas kernels for 3%

profile of v6, /device:TPU:1, one launch (start us, length us, event | category | flops | bytes accessed | tf_op | source)
XLA Modules:
  0.0 32.1 jit_solution(5474668935038542940)
XLA Ops:
  0.0 1.8 %prepare.1 = (f32[16,16,512]{2,1,0:T(8,128)S(1)}, f32[256,128]{1,0:T(8,128)}) custom-call(f32[16,16,512]{2,1,0:T(8,128)} %bitcast.7), custom_call_target="tpu_custom_call" | custom-call | tf_op jit(solution)/shard_map/prepare/pallas_call | solution.py:330
  1.8 15.7 %all-to-all-start = ((f32[256,1,128]{2,1,0:T(1,128)}), f32[256,1,128]{2,1,0:T(1,128)S(1)}, u32[]{:S(2)}, u32[]{:S(2)}) async-start(f32[256,1,128]{2,1,0:T(1,128)} %bitcast.2), calls=%async_computation | async-start | bytes 262144 | tf_op jit(solution)/shard_map/all_to_all | solution.py:369
  17.5 0.4 %rows.1 = (f32[80,128]{1,0:T(8,128)S(1)}, f32[80,128]{1,0:T(8,128)S(1)}) custom-call(f32[16,16,512]{2,1,0:T(8,128)S(1)} %get-tuple-element.13.raw_ref), custom_call_target="tpu_custom_call" | custom-call | tf_op jit(solution)/shard_map/rows/pallas_call | solution.py:339
  17.9 1.7 %collective-permute-start = (f32[80,128]{1,0:T(8,128)S(1)}, f32[80,128]{1,0:T(8,128)S(1)}, u32[]{:S(2)}, u32[]{:S(2)}) collective-permute-start(f32[80,128]{1,0:T(8,128)S(1)} %get-tuple-element.14), channel_id=1, source_target_pairs={{0,7},{1,2},{2,1},{3,4},{4,3},{5,6},{6,5},{7,0},{8,15},{9,10},{10,... | collective-permute-start | bytes 122888 | tf_op jit(solution)/shard_map/ppermute | solution.py:367
  19.6 1.4 %collective-permute-start.1 = (f32[80,128]{1,0:T(8,128)S(1)}, f32[80,128]{1,0:T(8,128)S(1)}, u32[]{:S(2)}, u32[]{:S(2)}) collective-permute-start(f32[80,128]{1,0:T(8,128)S(1)} %get-tuple-element.15), channel_id=1, source_target_pairs={{0,1},{1,0},{2,3},{3,2},{4,5},{5,4},{6,7},{7,6},{8,9},{9,8},{10,11... | collective-permute-start | bytes 122888 | tf_op jit(solution)/shard_map/ppermute | solution.py:367
  20.9 0.5 %split.1.phase_ref = f32[4,256,128]{2,1,0:T(8,128)S(1)} custom-call(f32[16,16,512]{2,1,0:T(8,128)S(1)} %get-tuple-element.13.raw_ref), custom_call_target="tpu_custom_call" | custom-call | tf_op jit(solution)/shard_map/split/pallas_call | solution.py:352
  21.5 0.3 collective-permute-done.yfar_ref
  21.7 0.1 collective-permute-done.1.ynear_ref
  21.9 1.5 %collective-permute-start.2 = (f32[80,128]{1,0:T(8,128)S(1)}, f32[80,128]{1,0:T(8,128)S(1)}, u32[]{:S(2)}, u32[]{:S(2)}) collective-permute-start(f32[80,128]{1,0:T(8,128)S(1)} %get-tuple-element.18), channel_id=1, source_target_pairs={{0,8},{8,16},{16,24},{24,32},{32,40},{40,48},{48,56},{56,64},{64,7... | collective-permute-start | bytes 122888 | tf_op jit(solution)/shard_map/ppermute | solution.py:363
  23.4 5.3 %collective-permute-start.3 = (f32[80,128]{1,0:T(8,128)S(1)}, f32[80,128]{1,0:T(8,128)S(1)}, u32[]{:S(2)}, u32[]{:S(2)}) collective-permute-start(f32[80,128]{1,0:T(8,128)S(1)} %get-tuple-element.19), channel_id=1, source_target_pairs={{0,248},{8,0},{16,8},{24,16},{32,24},{40,32},{48,40},{56,48},{64,5... | collective-permute-start | bytes 122888 | tf_op jit(solution)/shard_map/ppermute | solution.py:363
  28.7 1.6 %collective-permute-done.2.xlow_ref = f32[80,128]{1,0:T(8,128)S(1)} collective-permute-done((f32[80,128]{1,0:T(8,128)S(1)}, f32[80,128]{1,0:T(8,128)S(1)}, u32[]{:S(2)}, u32[]{:S(2)}) %collective-permute-start.2) | collective-permute-done | bytes 40992 | tf_op jit(solution)/shard_map/ppermute | solution.py:363
  30.3 0.0 collective-permute-done.3.xhigh_ref
  30.3 0.0 all-to-all-done
  30.3 1.8 %compress.1 = f32[16,16,512]{2,1,0:T(8,128)} custom-call(f32[4,256,128]{2,1,0:T(8,128)S(1)} %split.1.phase_ref, f32[80,128]{1,0:T(8,128)S(1)} %get-tuple-element.16.ylow_ref, f32[80,128]{1,0:T(8,128)S(1)} %get-tuple-element.17.yhigh_ref, f32[80,128]{1,0:T(8,128)S(1)} %collective-permute-done.2.xlow_ref, f32[80,128]{1,0:T(8,128)S(1)} %collective-permute-done.3.xhigh_ref, ...), custom_call_target="tpu_custom_call" | custom-call | tf_op jit(solution)/shard_map/compress/pallas_call | solution.py:387
  (1 shorter events, 0.0 us)
Async XLA Ops:
  1.8 28.4 %all-to-all-start = ((f32[256,1,128]{2,1,0:T(1,128)}), f32[256,1,128]{2,1,0:T(1,128)S(1)}, u32[]{:S(2)}, u32[]{:S(2)}) async-start(f32[256,1,128]{2,1,0:T(1,128)} %bitcast.2), calls=%async_computation | async-start | bytes 262144 | tf_op jit(solution)/shard_map/all_to_all | solution.py:369
  17.9 3.9 %collective-permute-start = (f32[80,128]{1,0:T(8,128)S(1)}, f32[80,128]{1,0:T(8,128)S(1)}, u32[]{:S(2)}, u32[]{:S(2)}) collective-permute-start(f32[80,128]{1,0:T(8,128)S(1)} %get-tuple-element.14), channel_id=1, source_target_pairs={{0,7},{1,2},{2,1},{3,4},{4,3},{5,6},{6,5},{7,0},{8,15},{9,10},{10,... | collective-permute-start | bytes 122888 | tf_op jit(solution)/shard_map/ppermute | solution.py:367
  19.6 2.2 %collective-permute-start.1 = (f32[80,128]{1,0:T(8,128)S(1)}, f32[80,128]{1,0:T(8,128)S(1)}, u32[]{:S(2)}, u32[]{:S(2)}) collective-permute-start(f32[80,128]{1,0:T(8,128)S(1)} %get-tuple-element.15), channel_id=1, source_target_pairs={{0,1},{1,0},{2,3},{3,2},{4,5},{5,4},{6,7},{7,6},{8,9},{9,8},{10,11... | collective-permute-start | bytes 122888 | tf_op jit(solution)/shard_map/ppermute | solution.py:367
  21.9 8.4 %collective-permute-start.2 = (f32[80,128]{1,0:T(8,128)S(1)}, f32[80,128]{1,0:T(8,128)S(1)}, u32[]{:S(2)}, u32[]{:S(2)}) collective-permute-start(f32[80,128]{1,0:T(8,128)S(1)} %get-tuple-element.18), channel_id=1, source_target_pairs={{0,8},{8,16},{16,24},{24,32},{32,40},{40,48},{48,56},{56,64},{64,7... | collective-permute-start | bytes 122888 | tf_op jit(solution)/shard_map/ppermute | solution.py:363
  23.4 6.9 %collective-permute-start.3 = (f32[80,128]{1,0:T(8,128)S(1)}, f32[80,128]{1,0:T(8,128)S(1)}, u32[]{:S(2)}, u32[]{:S(2)}) collective-permute-start(f32[80,128]{1,0:T(8,128)S(1)} %get-tuple-element.19), channel_id=1, source_target_pairs={{0,248},{8,0},{16,8},{24,16},{32,24},{40,32},{48,40},{56,48},{64,5... | collective-permute-start | bytes 122888 | tf_op jit(solution)/shard_map/ppermute | solution.py:363

commit v7 on v6

--- a/solution.py
+++ b/solution.py
@@ -62,7 +62,7 @@
     return pieces
 
 
-LOW_PIECES = plane_pieces(LOW_PLANES, TOTAL)
+LOW_PIECES = plane_pieces(LOW_PLANES, 48)
 HIGH_PIECES = plane_pieces(HIGH_PLANES, TOTAL)
 
 
@@ -174,6 +174,10 @@
                         ref[r : r + 1, :] = source[at + x // step : at + x // step + 1, :]
         for i, z, x, first, count, step, at in pieces:
             out[at : at + count, :] = ref[row_slice(ROWS * i + first, count, step), :]
+
+
+def relay_kernel(source_ref, target_ref):
+    target_ref[...] = source_ref[...]
 
 
 def merge_phases(parts, lane):
@@ -373,7 +377,7 @@
         join_kernel,
         in_specs=[vmem] * 3,
         out_specs=[vmem] * 4,
-        out_shape=[shape(TOTAL, 128)] * 4,
+        out_shape=[shape(48, 128)] + [shape(TOTAL, 128)] * 3,
         scratch_shapes=[
             pltpu.VMEM((ROWS * len(LOW_PLANES), 128), F32),
             pltpu.VMEM((ROWS * len(HIGH_PLANES), 128), F32),
@@ -384,6 +388,15 @@
     xlow = shifted(low, "gx", 1)
     xhigh = shifted(high, "gx", -1)
 
+    xlow = pl.pallas_call(
+        relay_kernel,
+        in_specs=[vmem],
+        out_specs=vmem,
+        out_shape=shape(48, 128),
+        compiler_params=params,
+        cost_estimate=pl.CostEstimate(flops=2 * 10**9, bytes_accessed=10**6, transcendentals=0),
+        name="relay",
+    )(xlow)
     codes = pl.pallas_call(
         compress_kernel,
         in_specs=[vmem] * 6,

time: 32.2 us -> 32.2 us (level)
  transfers between devices with their start and end apart: 5 -> 5, of which waited for: 3 -> 4; matrix products, arithmetic and copies ran while one was open for 0% -> 0% of each run, Pallas kernels for 3% -> 3%
where the time goes in v7:
time: 32.2 us; the launch traced here: 32 us
  starting transfers between devices  25.6 us (80%)
  Pallas kernels  4.56 us (14%)
  waiting for transfers between devices  1.89 us (6%)
    all_to_all x1, starting transfers between devices, shards(): peaks = lax.all_to_all(peak, AXES, 0, 0, tiled=True)  15.7 us
    ppermute x2, starting transfers between devices, shifted(): return lax.ppermute(array, axis, [(i, (i + d) % n) for i in range(n)])  6.81 us
    ppermute x2, starting transfers between devices, exchanged(): lax.ppermute(array, axis, [(i, (i + (1 if i % 2 == odd else -1)) % n) for...  3.08 us
    pallas_call x1, Pallas kernels, shards(): pl.pallas_call(compress_kernel, in_specs=[vmem] * 6, out_specs=hbm, out_s...  1.82 us
    pallas_call x1, Pallas kernels, shards(): pl.pallas_call(prepare_kernel, in_specs=[hbm], out_specs=[vmem, hbm], out...  1.81 us
    ppermute x2, waiting for transfers between devices, shifted(): return lax.ppermute(array, axis, [(i, (i + d) % n) for i in range(n)])  1.42 us
  transfers between devices with their start and end apart: 5, of which 4 were waited for; matrix products, arithmetic and copies ran while one was open for 0% of the time, Pallas kernels for 3%

profile of v7, /device:TPU:1, one launch (start us, length us, event | category | flops | bytes accessed | tf_op | source)
XLA Modules:
  0.0 32.0 jit_solution(11509368381370592088)
XLA Ops:
  0.0 1.8 %prepare.1 = (f32[16,16,512]{2,1,0:T(8,128)S(1)}, f32[256,128]{1,0:T(8,128)}) custom-call(f32[16,16,512]{2,1,0:T(8,128)} %bitcast.7), custom_call_target="tpu_custom_call" | custom-call | tf_op jit(solution)/shard_map/prepare/pallas_call | solution.py:334
  1.8 15.7 %all-to-all-start = ((f32[256,1,128]{2,1,0:T(1,128)}), f32[256,1,128]{2,1,0:T(1,128)S(1)}, u32[]{:S(2)}, u32[]{:S(2)}) async-start(f32[256,1,128]{2,1,0:T(1,128)} %bitcast.2), calls=%async_computation | async-start | bytes 262144 | tf_op jit(solution)/shard_map/all_to_all | solution.py:373
  17.5 0.4 %rows.1 = (f32[80,128]{1,0:T(8,128)S(1)}, f32[80,128]{1,0:T(8,128)S(1)}) custom-call(f32[16,16,512]{2,1,0:T(8,128)S(1)} %get-tuple-element.13.raw_ref), custom_call_target="tpu_custom_call" | custom-call | tf_op jit(solution)/shard_map/rows/pallas_call | solution.py:343
  17.9 1.7 %collective-permute-start = (f32[80,128]{1,0:T(8,128)S(1)}, f32[80,128]{1,0:T(8,128)S(1)}, u32[]{:S(2)}, u32[]{:S(2)}) collective-permute-start(f32[80,128]{1,0:T(8,128)S(1)} %get-tuple-element.14), channel_id=1, source_target_pairs={{0,7},{1,2},{2,1},{3,4},{4,3},{5,6},{6,5},{7,0},{8,15},{9,10},{10,... | collective-permute-start | bytes 122888 | tf_op jit(solution)/shard_map/ppermute | solution.py:371
  19.6 1.4 %collective-permute-start.1 = (f32[80,128]{1,0:T(8,128)S(1)}, f32[80,128]{1,0:T(8,128)S(1)}, u32[]{:S(2)}, u32[]{:S(2)}) collective-permute-start(f32[80,128]{1,0:T(8,128)S(1)} %get-tuple-element.15), channel_id=1, source_target_pairs={{0,1},{1,0},{2,3},{3,2},{4,5},{5,4},{6,7},{7,6},{8,9},{9,8},{10,11... | collective-permute-start | bytes 122888 | tf_op jit(solution)/shard_map/ppermute | solution.py:371
  20.9 0.5 %split.1.phase_ref = f32[4,256,128]{2,1,0:T(8,128)S(1)} custom-call(f32[16,16,512]{2,1,0:T(8,128)S(1)} %get-tuple-element.13.raw_ref), custom_call_target="tpu_custom_call" | custom-call | tf_op jit(solution)/shard_map/split/pallas_call | solution.py:356
  21.5 0.3 collective-permute-done.yfar_ref
  21.7 0.1 collective-permute-done.1.ynear_ref
  21.9 1.5 %collective-permute-start.2 = (f32[48,128]{1,0:T(8,128)S(1)}, f32[48,128]{1,0:T(8,128)S(1)}, u32[]{:S(2)}, u32[]{:S(2)}) collective-permute-start(f32[48,128]{1,0:T(8,128)S(1)} %get-tuple-element.18), channel_id=1, source_target_pairs={{0,8},{8,16},{16,24},{24,32},{32,40},{40,48},{48,56},{56,64},{64,7... | collective-permute-start | bytes 73736 | tf_op jit(solution)/shard_map/ppermute | solution.py:367
  23.4 5.3 %collective-permute-start.3 = (f32[80,128]{1,0:T(8,128)S(1)}, f32[80,128]{1,0:T(8,128)S(1)}, u32[]{:S(2)}, u32[]{:S(2)}) collective-permute-start(f32[80,128]{1,0:T(8,128)S(1)} %get-tuple-element.19), channel_id=1, source_target_pairs={{0,248},{8,0},{16,8},{24,16},{32,24},{40,32},{48,40},{56,48},{64,5... | collective-permute-start | bytes 122888 | tf_op jit(solution)/shard_map/ppermute | solution.py:367
  28.7 1.4 %collective-permute-done.2.source_ref = f32[48,128]{1,0:T(8,128)S(1)} collective-permute-done((f32[48,128]{1,0:T(8,128)S(1)}, f32[48,128]{1,0:T(8,128)S(1)}, u32[]{:S(2)}, u32[]{:S(2)}) %collective-permute-start.2) | collective-permute-done | bytes 24608 | tf_op jit(solution)/shard_map/ppermute | solution.py:367
  30.1 0.0 collective-permute-done.3.xhigh_ref
  30.1 0.1 all-to-all-done
  30.2 1.8 %compress.1 = f32[16,16,512]{2,1,0:T(8,128)} custom-call(f32[4,256,128]{2,1,0:T(8,128)S(1)} %split.1.phase_ref, f32[80,128]{1,0:T(8,128)S(1)} %get-tuple-element.16.ylow_ref, f32[80,128]{1,0:T(8,128)S(1)} %get-tuple-element.17.yhigh_ref, f32[48,128]{1,0:T(8,128)S(1)} %relay.1.xlow_ref, f32[80,128]{1,0:T(8,128)S(1)} %collective-permute-done.3.xhigh_ref, ...), custom_call_target="tpu_custom_call" | custom-call | tf_op jit(solution)/shard_map/compress/pallas_call | solution.py:400
  (2 shorter events, 0.0 us)
Async XLA Ops:
  1.8 28.4 %all-to-all-start = ((f32[256,1,128]{2,1,0:T(1,128)}), f32[256,1,128]{2,1,0:T(1,128)S(1)}, u32[]{:S(2)}, u32[]{:S(2)}) async-start(f32[256,1,128]{2,1,0:T(1,128)} %bitcast.2), calls=%async_computation | async-start | bytes 262144 | tf_op jit(solution)/shard_map/all_to_all | solution.py:373
  17.9 3.9 %collective-permute-start = (f32[80,128]{1,0:T(8,128)S(1)}, f32[80,128]{1,0:T(8,128)S(1)}, u32[]{:S(2)}, u32[]{:S(2)}) collective-permute-start(f32[80,128]{1,0:T(8,128)S(1)} %get-tuple-element.14), channel_id=1, source_target_pairs={{0,7},{1,2},{2,1},{3,4},{4,3},{5,6},{6,5},{7,0},{8,15},{9,10},{10,... | collective-permute-start | bytes 122888 | tf_op jit(solution)/shard_map/ppermute | solution.py:371
  19.6 2.2 %collective-permute-start.1 = (f32[80,128]{1,0:T(8,128)S(1)}, f32[80,128]{1,0:T(8,128)S(1)}, u32[]{:S(2)}, u32[]{:S(2)}) collective-permute-start(f32[80,128]{1,0:T(8,128)S(1)} %get-tuple-element.15), channel_id=1, source_target_pairs={{0,1},{1,0},{2,3},{3,2},{4,5},{5,4},{6,7},{7,6},{8,9},{9,8},{10,11... | collective-permute-start | bytes 122888 | tf_op jit(solution)/shard_map/ppermute | solution.py:371
  21.9 8.2 %collective-permute-start.2 = (f32[48,128]{1,0:T(8,128)S(1)}, f32[48,128]{1,0:T(8,128)S(1)}, u32[]{:S(2)}, u32[]{:S(2)}) collective-permute-start(f32[48,128]{1,0:T(8,128)S(1)} %get-tuple-element.18), channel_id=1, source_target_pairs={{0,8},{8,16},{16,24},{24,32},{32,40},{40,48},{48,56},{56,64},{64,7... | collective-permute-start | bytes 73736 | tf_op jit(solution)/shard_map/ppermute | solution.py:367
  23.4 6.7 %collective-permute-start.3 = (f32[80,128]{1,0:T(8,128)S(1)}, f32[80,128]{1,0:T(8,128)S(1)}, u32[]{:S(2)}, u32[]{:S(2)}) collective-permute-start(f32[80,128]{1,0:T(8,128)S(1)} %get-tuple-element.19), channel_id=1, source_target_pairs={{0,248},{8,0},{16,8},{24,16},{32,24},{40,32},{48,40},{56,48},{64,5... | collective-permute-start | bytes 122888 | tf_op jit(solution)/shard_map/ppermute | solution.py:367

commit v8 on v7

--- a/solution.py
+++ b/solution.py
@@ -197,9 +197,9 @@
     whole = jnp.round(scaled)
     r = scaled - whole
     s = r * r
-    q = Q_COEFFS[-1]
-    for c in Q_COEFFS[-2::-1]:
-        q = q * s + c
+    c0, c1, c2, c3, c4 = Q_COEFFS
+    ss = s * s
+    q = (c0 + c1 * s) + ss * ((c2 + c3 * s) + c4 * ss)
     return whole + (r * s) * q
 
 

time: 32.2 us -> 32.2 us (level)
  no operation moved by 1% of the time
where the time goes in v8:
time: 32.2 us; the launch traced here: 32 us
  starting transfers between devices  25.6 us (80%)
  Pallas kernels  4.57 us (14%)
  waiting for transfers between devices  1.89 us (6%)
    all_to_all x1, starting transfers between devices, shards(): peaks = lax.all_to_all(peak, AXES, 0, 0, tiled=True)  15.7 us
    ppermute x2, starting transfers between devices, shifted(): return lax.ppermute(array, axis, [(i, (i + d) % n) for i in range(n)])  6.81 us
    ppermute x2, starting transfers between devices, exchanged(): lax.ppermute(array, axis, [(i, (i + (1 if i % 2 == odd else -1)) % n) for...  3.08 us
    pallas_call x1, Pallas kernels, shards(): pl.pallas_call(compress_kernel, in_specs=[vmem] * 6, out_specs=hbm, out_s...  1.82 us
    pallas_call x1, Pallas kernels, shards(): pl.pallas_call(prepare_kernel, in_specs=[hbm], out_specs=[vmem, hbm], out...  1.81 us
    ppermute x2, waiting for transfers between devices, shifted(): return lax.ppermute(array, axis, [(i, (i + d) % n) for i in range(n)])  1.42 us
  transfers between devices with their start and end apart: 5, of which 4 were waited for; matrix products, arithmetic and copies ran while one was open for 0% of the time, Pallas kernels for 3%

profile of v8, /device:TPU:1, one launch (start us, length us, event | category | flops | bytes accessed | tf_op | source)
XLA Modules:
  0.0 32.0 jit_solution(7672986501315164152)
XLA Ops:
  0.0 1.8 %prepare.1 = (f32[16,16,512]{2,1,0:T(8,128)S(1)}, f32[256,128]{1,0:T(8,128)}) custom-call(f32[16,16,512]{2,1,0:T(8,128)} %bitcast.7), custom_call_target="tpu_custom_call" | custom-call | tf_op jit(solution)/shard_map/prepare/pallas_call | solution.py:334
  1.8 15.7 %all-to-all-start = ((f32[256,1,128]{2,1,0:T(1,128)}), f32[256,1,128]{2,1,0:T(1,128)S(1)}, u32[]{:S(2)}, u32[]{:S(2)}) async-start(f32[256,1,128]{2,1,0:T(1,128)} %bitcast.2), calls=%async_computation | async-start | bytes 262144 | tf_op jit(solution)/shard_map/all_to_all | solution.py:373
  17.5 0.4 %rows.1 = (f32[80,128]{1,0:T(8,128)S(1)}, f32[80,128]{1,0:T(8,128)S(1)}) custom-call(f32[16,16,512]{2,1,0:T(8,128)S(1)} %get-tuple-element.13.raw_ref), custom_call_target="tpu_custom_call" | custom-call | tf_op jit(solution)/shard_map/rows/pallas_call | solution.py:343
  17.9 1.7 %collective-permute-start = (f32[80,128]{1,0:T(8,128)S(1)}, f32[80,128]{1,0:T(8,128)S(1)}, u32[]{:S(2)}, u32[]{:S(2)}) collective-permute-start(f32[80,128]{1,0:T(8,128)S(1)} %get-tuple-element.14), channel_id=1, source_target_pairs={{0,7},{1,2},{2,1},{3,4},{4,3},{5,6},{6,5},{7,0},{8,15},{9,10},{10,... | collective-permute-start | bytes 122888 | tf_op jit(solution)/shard_map/ppermute | solution.py:371
  19.6 1.4 %collective-permute-start.1 = (f32[80,128]{1,0:T(8,128)S(1)}, f32[80,128]{1,0:T(8,128)S(1)}, u32[]{:S(2)}, u32[]{:S(2)}) collective-permute-start(f32[80,128]{1,0:T(8,128)S(1)} %get-tuple-element.15), channel_id=1, source_target_pairs={{0,1},{1,0},{2,3},{3,2},{4,5},{5,4},{6,7},{7,6},{8,9},{9,8},{10,11... | collective-permute-start | bytes 122888 | tf_op jit(solution)/shard_map/ppermute | solution.py:371
  20.9 0.5 %split.1.phase_ref = f32[4,256,128]{2,1,0:T(8,128)S(1)} custom-call(f32[16,16,512]{2,1,0:T(8,128)S(1)} %get-tuple-element.13.raw_ref), custom_call_target="tpu_custom_call" | custom-call | tf_op jit(solution)/shard_map/split/pallas_call | solution.py:356
  21.5 0.3 collective-permute-done.yfar_ref
  21.7 0.1 collective-permute-done.1.ynear_ref
  21.9 1.5 %collective-permute-start.2 = (f32[48,128]{1,0:T(8,128)S(1)}, f32[48,128]{1,0:T(8,128)S(1)}, u32[]{:S(2)}, u32[]{:S(2)}) collective-permute-start(f32[48,128]{1,0:T(8,128)S(1)} %get-tuple-element.18), channel_id=1, source_target_pairs={{0,8},{8,16},{16,24},{24,32},{32,40},{40,48},{48,56},{56,64},{64,7... | collective-permute-start | bytes 73736 | tf_op jit(solution)/shard_map/ppermute | solution.py:367
  23.4 5.3 %collective-permute-start.3 = (f32[80,128]{1,0:T(8,128)S(1)}, f32[80,128]{1,0:T(8,128)S(1)}, u32[]{:S(2)}, u32[]{:S(2)}) collective-permute-start(f32[80,128]{1,0:T(8,128)S(1)} %get-tuple-element.19), channel_id=1, source_target_pairs={{0,248},{8,0},{16,8},{24,16},{32,24},{40,32},{48,40},{56,48},{64,5... | collective-permute-start | bytes 122888 | tf_op jit(solution)/shard_map/ppermute | solution.py:367
  28.7 1.4 %collective-permute-done.2.source_ref = f32[48,128]{1,0:T(8,128)S(1)} collective-permute-done((f32[48,128]{1,0:T(8,128)S(1)}, f32[48,128]{1,0:T(8,128)S(1)}, u32[]{:S(2)}, u32[]{:S(2)}) %collective-permute-start.2) | collective-permute-done | bytes 24608 | tf_op jit(solution)/shard_map/ppermute | solution.py:367
  30.1 0.0 collective-permute-done.3.xhigh_ref
  30.1 0.1 all-to-all-done
  30.2 1.8 %compress.1 = f32[16,16,512]{2,1,0:T(8,128)} custom-call(f32[4,256,128]{2,1,0:T(8,128)S(1)} %split.1.phase_ref, f32[80,128]{1,0:T(8,128)S(1)} %get-tuple-element.16.ylow_ref, f32[80,128]{1,0:T(8,128)S(1)} %get-tuple-element.17.yhigh_ref, f32[48,128]{1,0:T(8,128)S(1)} %relay.1.xlow_ref, f32[80,128]{1,0:T(8,128)S(1)} %collective-permute-done.3.xhigh_ref, ...), custom_call_target="tpu_custom_call" | custom-call | tf_op jit(solution)/shard_map/compress/pallas_call | solution.py:400
  (2 shorter events, 0.0 us)
Async XLA Ops:
  1.8 28.4 %all-to-all-start = ((f32[256,1,128]{2,1,0:T(1,128)}), f32[256,1,128]{2,1,0:T(1,128)S(1)}, u32[]{:S(2)}, u32[]{:S(2)}) async-start(f32[256,1,128]{2,1,0:T(1,128)} %bitcast.2), calls=%async_computation | async-start | bytes 262144 | tf_op jit(solution)/shard_map/all_to_all | solution.py:373
  17.9 3.9 %collective-permute-start = (f32[80,128]{1,0:T(8,128)S(1)}, f32[80,128]{1,0:T(8,128)S(1)}, u32[]{:S(2)}, u32[]{:S(2)}) collective-permute-start(f32[80,128]{1,0:T(8,128)S(1)} %get-tuple-element.14), channel_id=1, source_target_pairs={{0,7},{1,2},{2,1},{3,4},{4,3},{5,6},{6,5},{7,0},{8,15},{9,10},{10,... | collective-permute-start | bytes 122888 | tf_op jit(solution)/shard_map/ppermute | solution.py:371
  19.6 2.2 %collective-permute-start.1 = (f32[80,128]{1,0:T(8,128)S(1)}, f32[80,128]{1,0:T(8,128)S(1)}, u32[]{:S(2)}, u32[]{:S(2)}) collective-permute-start(f32[80,128]{1,0:T(8,128)S(1)} %get-tuple-element.15), channel_id=1, source_target_pairs={{0,1},{1,0},{2,3},{3,2},{4,5},{5,4},{6,7},{7,6},{8,9},{9,8},{10,11... | collective-permute-start | bytes 122888 | tf_op jit(solution)/shard_map/ppermute | solution.py:371
  21.9 8.2 %collective-permute-start.2 = (f32[48,128]{1,0:T(8,128)S(1)}, f32[48,128]{1,0:T(8,128)S(1)}, u32[]{:S(2)}, u32[]{:S(2)}) collective-permute-start(f32[48,128]{1,0:T(8,128)S(1)} %get-tuple-element.18), channel_id=1, source_target_pairs={{0,8},{8,16},{16,24},{24,32},{32,40},{40,48},{48,56},{56,64},{64,7... | collective-permute-start | bytes 73736 | tf_op jit(solution)/shard_map/ppermute | solution.py:367
  23.4 6.7 %collective-permute-start.3 = (f32[80,128]{1,0:T(8,128)S(1)}, f32[80,128]{1,0:T(8,128)S(1)}, u32[]{:S(2)}, u32[]{:S(2)}) collective-permute-start(f32[80,128]{1,0:T(8,128)S(1)} %get-tuple-element.19), channel_id=1, source_target_pairs={{0,248},{8,0},{16,8},{24,16},{32,24},{40,32},{48,40},{56,48},{64,5... | collective-permute-start | bytes 122888 | tf_op jit(solution)/shard_map/ppermute | solution.py:367

commit v9 on v7

--- a/solution.py
+++ b/solution.py
@@ -229,9 +229,10 @@
         for _, z, x, first, count, step, at in pieces:
             known[z][row_slice(plane(x + shift) + first, count, step), :] = source[at : at + count, :]
 
-    peaks = peaks_ref[0:8, :]
-    for i in range(1, peaks_ref.shape[0] // 8):
-        peaks = jnp.maximum(peaks, peaks_ref[8 * i : 8 * i + 8, :])
+    parts = [peaks_ref[8 * i : 8 * i + 8, :] for i in range(peaks_ref.shape[0] // 8)]
+    while len(parts) > 1:
+        parts = [jnp.maximum(p, q) for p, q in zip(parts[::2], parts[1::2])]
+    peaks = parts[0]
     upper = jnp.max(jnp.where(lane < 64, peaks, -jnp.inf))
     lower = jnp.max(jnp.where(lane < 64, -jnp.inf, peaks))
     step = jnp.full((1, 1), 2.0 * (REL_BOUND * (upper + lower)), F32)

time: 32.2 us -> 32.2 us (level)
  no operation moved by 1% of the time
where the time goes in v9:
time: 32.2 us; the launch traced here: 32 us
  starting transfers between devices  25.6 us (80%)
  Pallas kernels  4.55 us (14%)
  waiting for transfers between devices  1.89 us (6%)
    all_to_all x1, starting transfers between devices, shards(): peaks = lax.all_to_all(peak, AXES, 0, 0, tiled=True)  15.7 us
    ppermute x2, starting transfers between devices, shifted(): return lax.ppermute(array, axis, [(i, (i + d) % n) for i in range(n)])  6.81 us
    ppermute x2, starting transfers between devices, exchanged(): lax.ppermute(array, axis, [(i, (i + (1 if i % 2 == odd else -1)) % n) for...  3.08 us
    pallas_call x1, Pallas kernels, shards(): pl.pallas_call(compress_kernel, in_specs=[vmem] * 6, out_specs=hbm, out_s...  1.81 us
    pallas_call x1, Pallas kernels, shards(): pl.pallas_call(prepare_kernel, in_specs=[hbm], out_specs=[vmem, hbm], out...  1.81 us
    ppermute x2, waiting for transfers between devices, shifted(): return lax.ppermute(array, axis, [(i, (i + d) % n) for i in range(n)])  1.42 us
  transfers between devices with their start and end apart: 5, of which 4 were waited for; matrix products, arithmetic and copies ran while one was open for 0% of the time, Pallas kernels for 3%

profile of v9, /device:TPU:1, one launch (start us, length us, event | category | flops | bytes accessed | tf_op | source)
XLA Modules:
  0.0 32.0 jit_solution(7436689422757651089)
XLA Ops:
  0.0 1.8 %prepare.1 = (f32[16,16,512]{2,1,0:T(8,128)S(1)}, f32[256,128]{1,0:T(8,128)}) custom-call(f32[16,16,512]{2,1,0:T(8,128)} %bitcast.7), custom_call_target="tpu_custom_call" | custom-call | tf_op jit(solution)/shard_map/prepare/pallas_call | solution.py:335
  1.8 15.7 %all-to-all-start = ((f32[256,1,128]{2,1,0:T(1,128)}), f32[256,1,128]{2,1,0:T(1,128)S(1)}, u32[]{:S(2)}, u32[]{:S(2)}) async-start(f32[256,1,128]{2,1,0:T(1,128)} %bitcast.2), calls=%async_computation | async-start | bytes 262144 | tf_op jit(solution)/shard_map/all_to_all | solution.py:374
  17.5 0.4 %rows.1 = (f32[80,128]{1,0:T(8,128)S(1)}, f32[80,128]{1,0:T(8,128)S(1)}) custom-call(f32[16,16,512]{2,1,0:T(8,128)S(1)} %get-tuple-element.13.raw_ref), custom_call_target="tpu_custom_call" | custom-call | tf_op jit(solution)/shard_map/rows/pallas_call | solution.py:344
  17.9 1.7 %collective-permute-start = (f32[80,128]{1,0:T(8,128)S(1)}, f32[80,128]{1,0:T(8,128)S(1)}, u32[]{:S(2)}, u32[]{:S(2)}) collective-permute-start(f32[80,128]{1,0:T(8,128)S(1)} %get-tuple-element.14), channel_id=1, source_target_pairs={{0,7},{1,2},{2,1},{3,4},{4,3},{5,6},{6,5},{7,0},{8,15},{9,10},{10,... | collective-permute-start | bytes 122888 | tf_op jit(solution)/shard_map/ppermute | solution.py:372
  19.6 1.4 %collective-permute-start.1 = (f32[80,128]{1,0:T(8,128)S(1)}, f32[80,128]{1,0:T(8,128)S(1)}, u32[]{:S(2)}, u32[]{:S(2)}) collective-permute-start(f32[80,128]{1,0:T(8,128)S(1)} %get-tuple-element.15), channel_id=1, source_target_pairs={{0,1},{1,0},{2,3},{3,2},{4,5},{5,4},{6,7},{7,6},{8,9},{9,8},{10,11... | collective-permute-start | bytes 122888 | tf_op jit(solution)/shard_map/ppermute | solution.py:372
  20.9 0.5 %split.1.phase_ref = f32[4,256,128]{2,1,0:T(8,128)S(1)} custom-call(f32[16,16,512]{2,1,0:T(8,128)S(1)} %get-tuple-element.13.raw_ref), custom_call_target="tpu_custom_call" | custom-call | tf_op jit(solution)/shard_map/split/pallas_call | solution.py:357
  21.5 0.3 collective-permute-done.yfar_ref
  21.7 0.1 collective-permute-done.1.ynear_ref
  21.9 1.5 %collective-permute-start.2 = (f32[48,128]{1,0:T(8,128)S(1)}, f32[48,128]{1,0:T(8,128)S(1)}, u32[]{:S(2)}, u32[]{:S(2)}) collective-permute-start(f32[48,128]{1,0:T(8,128)S(1)} %get-tuple-element.18), channel_id=1, source_target_pairs={{0,8},{8,16},{16,24},{24,32},{32,40},{40,48},{48,56},{56,64},{64,7... | collective-permute-start | bytes 73736 | tf_op jit(solution)/shard_map/ppermute | solution.py:368
  23.4 5.3 %collective-permute-start.3 = (f32[80,128]{1,0:T(8,128)S(1)}, f32[80,128]{1,0:T(8,128)S(1)}, u32[]{:S(2)}, u32[]{:S(2)}) collective-permute-start(f32[80,128]{1,0:T(8,128)S(1)} %get-tuple-element.19), channel_id=1, source_target_pairs={{0,248},{8,0},{16,8},{24,16},{32,24},{40,32},{48,40},{56,48},{64,5... | collective-permute-start | bytes 122888 | tf_op jit(solution)/shard_map/ppermute | solution.py:368
  28.7 1.4 %collective-permute-done.2.source_ref = f32[48,128]{1,0:T(8,128)S(1)} collective-permute-done((f32[48,128]{1,0:T(8,128)S(1)}, f32[48,128]{1,0:T(8,128)S(1)}, u32[]{:S(2)}, u32[]{:S(2)}) %collective-permute-start.2) | collective-permute-done | bytes 24608 | tf_op jit(solution)/shard_map/ppermute | solution.py:368
  30.1 0.0 collective-permute-done.3.xhigh_ref
  30.1 0.1 all-to-all-done
  30.2 1.8 %compress.1 = f32[16,16,512]{2,1,0:T(8,128)} custom-call(f32[4,256,128]{2,1,0:T(8,128)S(1)} %split.1.phase_ref, f32[80,128]{1,0:T(8,128)S(1)} %get-tuple-element.16.ylow_ref, f32[80,128]{1,0:T(8,128)S(1)} %get-tuple-element.17.yhigh_ref, f32[48,128]{1,0:T(8,128)S(1)} %relay.1.xlow_ref, f32[80,128]{1,0:T(8,128)S(1)} %collective-permute-done.3.xhigh_ref, ...), custom_call_target="tpu_custom_call" | custom-call | tf_op jit(solution)/shard_map/compress/pallas_call | solution.py:401
  (2 shorter events, 0.0 us)
Async XLA Ops:
  1.8 28.4 %all-to-all-start = ((f32[256,1,128]{2,1,0:T(1,128)}), f32[256,1,128]{2,1,0:T(1,128)S(1)}, u32[]{:S(2)}, u32[]{:S(2)}) async-start(f32[256,1,128]{2,1,0:T(1,128)} %bitcast.2), calls=%async_computation | async-start | bytes 262144 | tf_op jit(solution)/shard_map/all_to_all | solution.py:374
  17.9 3.9 %collective-permute-start = (f32[80,128]{1,0:T(8,128)S(1)}, f32[80,128]{1,0:T(8,128)S(1)}, u32[]{:S(2)}, u32[]{:S(2)}) collective-permute-start(f32[80,128]{1,0:T(8,128)S(1)} %get-tuple-element.14), channel_id=1, source_target_pairs={{0,7},{1,2},{2,1},{3,4},{4,3},{5,6},{6,5},{7,0},{8,15},{9,10},{10,... | collective-permute-start | bytes 122888 | tf_op jit(solution)/shard_map/ppermute | solution.py:372
  19.6 2.2 %collective-permute-start.1 = (f32[80,128]{1,0:T(8,128)S(1)}, f32[80,128]{1,0:T(8,128)S(1)}, u32[]{:S(2)}, u32[]{:S(2)}) collective-permute-start(f32[80,128]{1,0:T(8,128)S(1)} %get-tuple-element.15), channel_id=1, source_target_pairs={{0,1},{1,0},{2,3},{3,2},{4,5},{5,4},{6,7},{7,6},{8,9},{9,8},{10,11... | collective-permute-start | bytes 122888 | tf_op jit(solution)/shard_map/ppermute | solution.py:372
  21.9 8.2 %collective-permute-start.2 = (f32[48,128]{1,0:T(8,128)S(1)}, f32[48,128]{1,0:T(8,128)S(1)}, u32[]{:S(2)}, u32[]{:S(2)}) collective-permute-start(f32[48,128]{1,0:T(8,128)S(1)} %get-tuple-element.18), channel_id=1, source_target_pairs={{0,8},{8,16},{16,24},{24,32},{32,40},{40,48},{48,56},{56,64},{64,7... | collective-permute-start | bytes 73736 | tf_op jit(solution)/shard_map/ppermute | solution.py:368
  23.4 6.7 %collective-permute-start.3 = (f32[80,128]{1,0:T(8,128)S(1)}, f32[80,128]{1,0:T(8,128)S(1)}, u32[]{:S(2)}, u32[]{:S(2)}) collective-permute-start(f32[80,128]{1,0:T(8,128)S(1)} %get-tuple-element.19), channel_id=1, source_target_pairs={{0,248},{8,0},{16,8},{24,16},{32,24},{40,32},{48,40},{56,48},{64,5... | collective-permute-start | bytes 122888 | tf_op jit(solution)/shard_map/ppermute | solution.py:368
